TPU v7x, 32 devices: a whole 2x2x4 slice. The times are simulated.
32 devices in a mesh: fsdp: 8 (over z, y), dp: 4 (over x, core).
Axes of the slice: x: 2, y: 2, z: 4, core: 2. Of those that a mesh axis runs over, the one named last changes fastest.
Arguments:
- tokens: bfloat16 [32768, 768], P(('fsdp', 'dp')), may hold values from -6 to 6
- cotangent: bfloat16 [32768, 768], P(('fsdp', 'dp')), may hold values from -6 to 6
- lengths: int32 [128], P(('fsdp', 'dp')), may hold values from 65 to 256, as said below
- buckets: int32 [128], P(('fsdp', 'dp')), may hold values from 0 to 1, as said below
- qkv_weight: bfloat16 [768, 2304], P('fsdp', 'dp'), may hold values from -0.21875 to 0.21875
- query_value_bias: bfloat16 [1536], P('fsdp'), may hold values from -1.5 to 1.5
- out_weight: bfloat16 [768, 768], P('fsdp', 'dp'), may hold values from -0.21875 to 0.21875
- out_bias: bfloat16 [768], P('fsdp'), may hold values from -1.5 to 1.5
- up_weight: bfloat16 [768, 3072], P('fsdp', 'dp'), may hold values from -0.21875 to 0.21875
- up_bias: bfloat16 [3072], P('fsdp'), may hold values from -1.5 to 1.5
- down_weight: bfloat16 [3072, 768], P('fsdp', 'dp'), may hold values from -0.109375 to 0.109375
- down_bias: bfloat16 [768], P('fsdp'), may hold values from -1.5 to 1.5
- first_gain: bfloat16 [768], P('fsdp'), may hold values from 0.5 to 1.5
- first_shift: bfloat16 [768], P('fsdp'), may hold values from -1.5 to 1.5
- mix_gain: bfloat16 [768], P('fsdp'), may hold values from 0.5 to 1.5
- mix_shift: bfloat16 [768], P('fsdp'), may hold values from -1.5 to 1.5
- second_gain: bfloat16 [768], P('fsdp'), may hold values from 0.5 to 1.5
- second_shift: bfloat16 [768], P('fsdp'), may hold values from -1.5 to 1.5
- hidden_gain: bfloat16 [3072], P('fsdp'), may hold values from 0.5 to 1.5
- hidden_shift: bfloat16 [3072], P('fsdp'), may hold values from -1.5 to 1.5
- head_scale: bfloat16 [12], replicated, may hold values from 0.5 to 2
- position_table: bfloat16 [1536, 12], P('fsdp'), may hold values from -4 to 4
Outputs:
- result_tokens: bfloat16 [32768, 768], P(('fsdp', 'dp'))
- input_grad: bfloat16 [32768, 768], P(('fsdp', 'dp'))
- qkv_weight_grad: float32 [768, 2304], P('fsdp', 'dp')
- query_value_bias_grad: float32 [1536], P('fsdp')
- out_weight_grad: float32 [768, 768], P('fsdp', 'dp')
- out_bias_grad: float32 [768], P('fsdp')
- up_weight_grad: float32 [768, 3072], P('fsdp', 'dp')
- up_bias_grad: float32 [3072], P('fsdp')
- down_weight_grad: float32 [3072, 768], P('fsdp', 'dp')
- down_bias_grad: float32 [768], P('fsdp')
- first_gain_grad: float32 [768], P('fsdp')
- first_shift_grad: float32 [768], P('fsdp')
- mix_gain_grad: float32 [768], P('fsdp')
- mix_shift_grad: float32 [768], P('fsdp')
- second_gain_grad: float32 [768], P('fsdp')
- second_shift_grad: float32 [768], P('fsdp')
- hidden_gain_grad: float32 [3072], P('fsdp')
- hidden_shift_grad: float32 [3072], P('fsdp')
- head_scale_grad: float32 [12], replicated
- position_table_grad: float32 [1536, 12], P('fsdp')
Inputs may be any that keep to these rules, and one draw needn't show every extreme that they name: `lengths`: sequence s holds its image's patches first (64 if buckets[s] is 0, 225 if it is 1) and one or more text tokens after them; one sequence in every draw has all 256 slots live. `buckets`: 0 for an image of 64 patches on an 8 x 8 grid, 1 for 225 patches on a 15 x 15 grid.
All inputs are finite; a program needn't handle non-finite values.
Results may differ from a plain program's by a relative error of at most 0.015.
Values may be sent and summed in bfloat16 or wider, within the bound.
A program may use at most 256 MiB of HBM per device.

v0:
```python
import functools

import jax
import jax.numpy as jnp
from jax import lax
from jax.experimental import pallas as pl
from jax.experimental.pallas import tpu as pltpu
from jax.sharding import PartitionSpec as P

D = 768
HEADS = 12
PAIRS = 6
HEAD_DIM = 64
FF = 3072
SLOT = 256
TABLE = 1536

EPS = 1e-05
MASKED = -1000000000.0
F32 = jnp.float32
BF16 = jnp.bfloat16
VMEM_LIMIT = 60 * 2**20
BACK_LIMIT = 60 * 2**20


def params(**more):
    return pltpu.CompilerParams(vmem_limit_bytes=VMEM_LIMIT, **more)


def nn(left, right):
    return lax.dot_general(left, right, (((1,), (0,)), ((), ())), preferred_element_type=F32)


def nt(left, right):
    return lax.dot_general(left, right, (((1,), (1,)), ((), ())), preferred_element_type=F32)


def standardize(values):
    center = values - jnp.mean(values, -1, keepdims=True)
    inverse = lax.rsqrt(jnp.mean(center * center, -1, keepdims=True) + EPS)
    return center * inverse, inverse


def norm_back(grad, unit, inverse):
    return inverse * (
        grad
        - jnp.mean(grad, -1, keepdims=True)
        - unit * jnp.mean(grad * unit, -1, keepdims=True)
    )


def column_sum(values):
    return jnp.sum(values, 0, keepdims=True)


def tall_sum(ref):
    def some(n, total):
        return total + column_sum(ref[rows_of(n, 64), :].astype(F32))

    return lax.fori_loop(0, ref.shape[0] // 64, some, jnp.zeros((1, ref.shape[1]), F32))


def split_low(values):
    high = values.astype(BF16)
    return high, (values - high.astype(F32)).astype(BF16)


def compaction(side, lanes):
    plane = lax.broadcasted_iota(jnp.int32, (1024, lanes), 0)
    lane = lax.broadcasted_iota(jnp.int32, (1024, lanes), 1)
    across = plane & 31
    return ((lane == side * (plane >> 5) + across) & (across < side)).astype(F32).astype(BF16)


def inside_grid(patches):
    row = lax.broadcasted_iota(jnp.int32, (SLOT, SLOT), 0)
    col = lax.broadcasted_iota(jnp.int32, (SLOT, SLOT), 1)
    return (row < patches) & (col < patches)


def store_tiles(ref, values):
    for k in range(ref.shape[0]):
        ref[k] = values[:, 128 * k : 128 * k + 128]


def load_tiles(ref):
    return jnp.concatenate([ref[k] for k in range(ref.shape[0])], 1)


def load_strided(ref, first, count):
    return jnp.concatenate(
        [ref[k, pl.ds(first, count, 16), :] for k in range(ref.shape[0])], 1
    )


def store_strided(ref, first, values):
    for k in range(ref.shape[0]):
        ref[k, pl.ds(first, values.shape[0], 16), :] = values[:, 128 * k : 128 * k + 128]


def bias_walls(table_ref, wall_small, wall_large, visual):
    plane = table_ref[:, 512:]
    shifted = [pltpu.roll(plane, (ic - 15) % 1024, 1) for ic in range(16)]
    stack = jnp.concatenate(shifted, 0).astype(BF16)
    store_tiles(wall_large, nn(stack, compaction(15, 512)))
    store_tiles(wall_small, nn(stack[:128], compaction(8, 256)))
    visual[...] = jnp.zeros_like(visual)


def bias_head(table_ref, out_ref, wall_small, wall_large, visual, h, carry):
    line = jnp.broadcast_to(table_ref[pl.ds(h, 1), :512], (SLOT, 512))
    textual = pltpu.roll(line, 257, 1, stride=1, stride_axis=0)[:, :SLOT]
    large = load_strided(wall_large, h, 16)
    for ir in range(15):
        visual[pl.ds(ir * 15, 16), :] = pltpu.roll(large, 512 - (15 - ir) * 15, 1)[:, :SLOT]
    out_ref[1, h] = jnp.where(inside_grid(225), visual[...], textual).astype(BF16)
    small = load_strided(wall_small, h, 8)
    rows = [pltpu.roll(small, 256 - (15 - ir) * 8, 1) for ir in range(8)]
    grid = jnp.concatenate(rows + [jnp.zeros((192, SLOT), F32)], 0)
    out_ref[0, h] = jnp.where(inside_grid(64), grid, textual).astype(BF16)
    return carry


def bias_kernel(table_ref, out_ref, wall_small, wall_large, visual):
    bias_walls(table_ref, wall_small, wall_large, visual)
    one_head = functools.partial(bias_head, table_ref, out_ref, wall_small, wall_large, visual)
    lax.fori_loop(0, HEADS, one_head, 0)


def build_bias(table):
    return pl.pallas_call(
        bias_kernel,
        out_shape=jax.ShapeDtypeStruct((2, HEADS, SLOT, SLOT), BF16),
        scratch_shapes=[
            pltpu.VMEM((2, 128, 128), F32),
            pltpu.VMEM((4, 256, 128), F32),
            pltpu.VMEM((SLOT, SLOT), F32),
        ],
        compiler_params=params(),
        name="build_bias",
    )(table)


def table_grad_start(out_ref, wall_small, wall_large):
    wall_small[...] = jnp.zeros_like(wall_small)
    wall_large[...] = jnp.zeros_like(wall_large)
    out_ref[...] = jnp.zeros_like(out_ref)


def table_grad_head(grid_ref, out_ref, wall_small, wall_large, h, slot):
    row = lax.broadcasted_iota(jnp.int32, (SLOT, SLOT), 0)
    col = lax.broadcasted_iota(jnp.int32, (SLOT, SLOT), 1)
    flip = (row + col == SLOT - 1).astype(F32).astype(BF16)
    lane = lax.broadcasted_iota(jnp.int32, (16, SLOT), 1)
    textual = jnp.where(inside_grid(64), 0.0, grid_ref[0, slot]) + jnp.where(
        inside_grid(225), 0.0, grid_ref[1, slot]
    )
    high, low = split_low(textual)
    flipped = nn(flip, high) + nn(flip, low)
    wide = jnp.concatenate([flipped, jnp.zeros((SLOT, SLOT), F32)], 1)
    out_ref[pl.ds(h, 1), :512] = column_sum(pltpu.roll(wide, 0, 1, stride=1, stride_axis=0))
    total = jnp.zeros((16, 512), F32)
    for ir in range(15):
        part = jnp.where(lane < 225, grid_ref[1, slot, pl.ds(ir * 15, 16), :], 0.0)
        part = jnp.concatenate([part, jnp.zeros((16, SLOT), F32)], 1)
        total = total + pltpu.roll(part, (15 - ir) * 15, 1)
    store_strided(wall_large, h, total)
    total = jnp.zeros((8, SLOT), F32)
    for ir in range(8):
        part = jnp.where(lane[:8] < 64, grid_ref[0, slot, pl.ds(ir * 8, 8), :], 0.0)
        total = total + pltpu.roll(part, (15 - ir) * 8, 1)
    store_strided(wall_small, h, total)


def table_grad_end(out_ref, wall_small, wall_large):
    high, low = split_low(load_tiles(wall_large))
    spread = compaction(15, 512)
    large = nt(high, spread) + nt(low, spread)
    high, low = split_low(load_tiles(wall_small))
    spread = compaction(8, 256)
    small = nt(high, spread) + nt(low, spread)
    plane = jnp.zeros((16, 1024), F32)
    for ic in range(15):
        part = large[ic * 16 : ic * 16 + 16]
        if ic < 8:
            part = part + small[ic * 16 : ic * 16 + 16]
        plane = plane + pltpu.roll(part, 15 - ic, 1)
    out_ref[:, 512:] = plane


def table_grad_kernel(grid_ref, out_ref, wall_small, wall_large):
    table_grad_start(out_ref, wall_small, wall_large)

    def one_head(h, carry):
        table_grad_head(grid_ref, out_ref, wall_small, wall_large, h, h)
        return carry

    lax.fori_loop(0, HEADS, one_head, 0)
    table_grad_end(out_ref, wall_small, wall_large)


def table_grad(grids):
    return pl.pallas_call(
        table_grad_kernel,
        out_shape=jax.ShapeDtypeStruct((16, TABLE), F32),
        scratch_shapes=[pltpu.VMEM((2, 128, 128), F32), pltpu.VMEM((4, 256, 128), F32)],
        compiler_params=params(),
        name="table_grad",
    )(grids)


def by_head(pair, axis):
    first = lax.broadcasted_iota(jnp.int32, pair.shape, 1) < HEAD_DIM
    return jnp.concatenate([jnp.where(first, pair, 0), jnp.where(first, 0, pair)], axis)


def attend(query, keys, values, bias, live):
    logits = nt(by_head(query, 0), keys)
    probs = []
    for half in range(2):
        rows = slice(SLOT * half, SLOT * half + SLOT)
        scores = jnp.where(live, logits[rows] + bias[half].astype(F32), MASKED)
        shifted = jnp.exp(scores - jnp.max(scores, -1, keepdims=True))
        probs.append((shifted * (1.0 / jnp.sum(shifted, -1, keepdims=True))).astype(BF16))
    return probs, nn(jnp.concatenate(probs, 1), by_head(values, 0))


def attend_back(query, keys, values, grad, probs):
    probs_grads = nt(by_head(grad, 0), values)
    grad_turned = grad.T
    query_turned = query.T
    keys_parts = []
    values_parts = []
    scores_grads = []
    lows = []
    for half in range(2):
        part = slice(HEAD_DIM * half, HEAD_DIM * half + HEAD_DIM)
        wide = probs[half].astype(F32)
        probs_grad = probs_grads[SLOT * half : SLOT * half + SLOT]
        values_parts.append(nn(grad_turned[part], probs[half]))
        scores_grad = wide * (probs_grad - jnp.sum(wide * probs_grad, -1, keepdims=True))
        scores_grads.append(scores_grad)
        lows.append(scores_grad.astype(BF16))
        keys_parts.append(nn(query_turned[part], lows[half]))
    query_grad = nn(jnp.concatenate(lows, 1), by_head(keys, 0)) * HEAD_DIM ** (-0.5)
    keys_grad = jnp.concatenate(keys_parts, 0).T
    values_grad = jnp.concatenate(values_parts, 0).T
    return query_grad.astype(BF16), keys_grad.astype(BF16), values_grad.astype(BF16), scores_grads


def attention_kernel(
    lengths, buckets, x_ref, vec_ref, weight_ref, qkv_bias_ref, bias_ref,
    normed_ref, qkv_ref, probs_ref, attended_ref,
):
    count = x_ref.shape[0] // SLOT

    def one_block(b, carry):
        rows = pl.ds(pl.multiple_of(b * SLOT, SLOT), SLOT)
        unit, inverse = standardize(x_ref[rows, :].astype(F32))
        normed_ref[rows, :] = (unit * vec_ref[0:1, :] + vec_ref[1:2, :]).astype(BF16)
        return carry

    lax.fori_loop(0, count, one_block, 0)

    def one_panel(n, carry):
        cols = pl.ds(pl.multiple_of(n * 256, 256), 256)
        out = nn(normed_ref[...], weight_ref[:, cols]) + qkv_bias_ref[:, cols]
        out = (out * jnp.where(n < 3, HEAD_DIM ** (-0.5), 1.0)).astype(BF16)
        qkv_ref[2 * n] = out[:, :128]
        qkv_ref[2 * n + 1] = out[:, 128:]
        return carry

    lax.fori_loop(0, 9, one_panel, 0)
    key_slot = lax.broadcasted_iota(jnp.int32, (SLOT, SLOT), 1)

    def one_unit(step, carry):
        pair = step // count
        s = step % count
        rows = pl.ds(pl.multiple_of(s * SLOT, SLOT), SLOT)
        bias = [bias_ref[buckets[s], 2 * pair + half] for half in range(2)]
        probs, out = attend(
            qkv_ref[pair, rows, :], qkv_ref[PAIRS + pair, rows, :], qkv_ref[2 * PAIRS + pair, rows, :],
            bias, key_slot < lengths[s],
        )
        for half in range(2):
            probs_ref[2 * pair + half, s] = probs[half]
        attended_ref[rows, pl.ds(pl.multiple_of(pair * 128, 128), 128)] = out
        return carry

    lax.fori_loop(0, PAIRS * count, one_unit, 0)


def attention(lengths, buckets, tokens, vecs, weight, qkv_bias, bias):
    rows = tokens.shape[0]
    count = rows // SLOT
    smem = pl.BlockSpec(memory_space=pltpu.SMEM)
    vmem = pl.BlockSpec(memory_space=pltpu.VMEM)
    return pl.pallas_call(
        attention_kernel,
        in_specs=[smem, smem] + [vmem] * 5,
        out_shape=[
            jax.ShapeDtypeStruct((rows, D), BF16),
            jax.ShapeDtypeStruct((3 * PAIRS, rows, 128), BF16),
            jax.ShapeDtypeStruct((HEADS, count, SLOT, SLOT), BF16),
            jax.ShapeDtypeStruct((rows, D), F32),
        ],
        compiler_params=params(),
        name="attention_forward",
    )(lengths, buckets, tokens, vecs, weight, qkv_bias, bias)


PANEL = 512


def feed_kernel(*refs):
    @pl.when(pl.program_id(0) == 0)
    def _():
        for ref in refs[17:19]:
            ref[...] = jnp.zeros_like(ref)

    feed_block(*refs, lambda: None)


def feed_block(
    x_ref, attended_ref, cot_ref, out_w, up_w, down_w, vec_ref, wide_ref, scale_ref,
    result_ref, mixed_ref, second_ref, act_ref, low_ref, branch_ref, middle_grad_ref,
    attended_low_ref, sums_ref, wide_sums_ref,
    gelu_ref, slope_ref, grad_ref, before_down,
):
    def add(row, values):
        sums_ref[row : row + 1, :] += column_sum(values)

    rows = x_ref.shape[0]
    attended = attended_ref[...]
    mix_unit, mix_inverse = standardize(attended * scale_ref[...])
    mixed = (mix_unit * vec_ref[2:3, :] + vec_ref[3:4, :]).astype(BF16)
    mixed_ref[...] = mixed
    middle = x_ref[...].astype(F32) + nn(mixed, out_w[...]) + vec_ref[6:7, :]
    second_unit, second_inverse = standardize(middle)
    second = (second_unit * vec_ref[4:5, :] + vec_ref[5:6, :]).astype(BF16)
    second_ref[...] = second
    cot = cot_ref[...]

    panels = [slice(n, n + PANEL) for n in range(0, FF, PANEL)]
    total = jnp.zeros((rows, 1), F32)
    for cols in panels:
        hidden = nn(second, up_w[:, cols]) + wide_ref[0:1, cols]
        cdf = 0.5 + 0.5 * lax.erf(hidden * 0.7071067811865476)
        gelu = hidden * cdf
        gelu_ref[:, cols] = gelu
        slope_ref[:, cols] = cdf + hidden * (jnp.exp(-0.5 * hidden * hidden) * 0.3989422804014327)
        total = total + jnp.sum(gelu, -1, keepdims=True)
    mean = total * (1.0 / FF)
    total = jnp.zeros((rows, 1), F32)
    for cols in panels:
        center = gelu_ref[:, cols] - mean
        total = total + jnp.sum(center * center, -1, keepdims=True)
    inverse = lax.rsqrt(total * (1.0 / FF) + EPS)
    before_down()
    result = middle + vec_ref[7:8, :]
    first = jnp.zeros((rows, 1), F32)
    second_moment = jnp.zeros((rows, 1), F32)
    for cols in panels:
        unit = (gelu_ref[:, cols] - mean) * inverse
        gelu_ref[:, cols] = unit
        act = (unit * wide_ref[1:2, cols] + wide_ref[2:3, cols]).astype(BF16)
        act_ref[:, cols] = act
        result = result + nt(act, down_w[:, cols])
        act_grad = nn(cot, down_w[:, cols])
        wide_sums_ref[1:2, cols] += column_sum(act_grad * unit)
        wide_sums_ref[2:3, cols] += column_sum(act_grad)
        grad = act_grad * wide_ref[1:2, cols]
        grad_ref[:, cols] = grad
        first = first + jnp.sum(grad, -1, keepdims=True)
        second_moment = second_moment + jnp.sum(grad * unit, -1, keepdims=True)
    result_ref[...] = result.astype(BF16)
    first = first * (1.0 / FF)
    second_moment = second_moment * (1.0 / FF)
    second_in = jnp.zeros((rows, D), F32)
    for cols in panels:
        grad = inverse * (grad_ref[:, cols] - first - gelu_ref[:, cols] * second_moment)
        low = (grad * slope_ref[:, cols]).astype(BF16)
        low_ref[:, cols] = low
        wide_sums_ref[0:1, cols] += column_sum(low.astype(F32))
        second_in = second_in + nt(low, up_w[:, cols])
    add(4, second_in * second_unit)
    add(5, second_in)
    cot_wide = cot.astype(F32)
    add(7, cot_wide)
    middle_grad = cot_wide + norm_back(second_in * vec_ref[4:5, :], second_unit, second_inverse)
    middle_grad_ref[...] = middle_grad
    branch = middle_grad.astype(BF16)
    branch_ref[...] = branch
    add(6, branch.astype(F32))
    mixed_in = nt(branch, out_w[...])
    add(2, mixed_in * mix_unit)
    add(3, mixed_in)
    grad = norm_back(mixed_in * vec_ref[2:3, :], mix_unit, mix_inverse)
    add(8, grad * attended)
    attended_low_ref[...] = (grad * scale_ref[...]).astype(BF16)


def feed_forward(tokens, attended, cotangent, out_w, up_w, down_w, vecs, wide, scales):
    rows = tokens.shape[0]
    tile = 256
    block = pl.BlockSpec((tile, D), lambda i: (i, 0))
    wide_block = pl.BlockSpec((tile, FF), lambda i: (i, 0))

    def whole(shape):
        return pl.BlockSpec(shape, lambda i: (0, 0), pipeline_mode=pl.Buffered(1))

    def held(shape):
        return pl.BlockSpec(shape, lambda i: (0, 0))

    return pl.pallas_call(
        feed_kernel,
        grid=(rows // tile,),
        in_specs=[block] * 3
        + [whole((D, D)), whole((D, FF)), whole((D, FF)), whole((8, D)), whole((8, FF)), whole((1, D))],
        out_specs=[block, block, block, wide_block, wide_block, block, block, block]
        + [held((16, D)), held((8, FF))],
        out_shape=[
            jax.ShapeDtypeStruct((rows, D), BF16),
            jax.ShapeDtypeStruct((rows, D), BF16),
            jax.ShapeDtypeStruct((rows, D), BF16),
            jax.ShapeDtypeStruct((rows, FF), BF16),
            jax.ShapeDtypeStruct((rows, FF), BF16),
            jax.ShapeDtypeStruct((rows, D), BF16),
            jax.ShapeDtypeStruct((rows, D), F32),
            jax.ShapeDtypeStruct((rows, D), BF16),
            jax.ShapeDtypeStruct((16, D), F32),
            jax.ShapeDtypeStruct((8, FF), F32),
        ],
        scratch_shapes=[pltpu.VMEM((tile, FF), F32)] * 3,
        compiler_params=params(dimension_semantics=("arbitrary",)),
        name="feed_forward",
    )(tokens, attended, cotangent, out_w, up_w, down_w, vecs, wide, scales)


def outer_kernel(left_ref, right_ref, out_ref, turned):
    @pl.when(pl.program_id(0) == 0)
    def _():
        turned[...] = left_ref[...].T

    out_ref[...] = nn(turned[...], right_ref[...]).astype(BF16)


def outer_product(left, right, panel):
    rows, width = left.shape
    cols = right.shape[1]
    return pl.pallas_call(
        outer_kernel,
        grid=(cols // panel,),
        in_specs=[
            pl.BlockSpec((rows, width), lambda i: (0, 0), pipeline_mode=pl.Buffered(1)),
            pl.BlockSpec((rows, panel), lambda i: (0, i)),
        ],
        out_specs=pl.BlockSpec((width, panel), lambda i: (0, i)),
        out_shape=jax.ShapeDtypeStruct((width, cols), BF16),
        scratch_shapes=[pltpu.VMEM((width, rows), BF16)],
        compiler_params=params(dimension_semantics=("arbitrary",)),
        name="weight_grad",
    )(left, right)


def attention_back_kernel(
    buckets, probs_ref, query_ref, keys_ref, values_ref, low_ref, normed_ref, x_ref, middle_ref,
    weight_q, weight_k, weight_v, vec_ref,
    input_grad_ref, grid_ref, weight_grad_ref, pair_ref, sums_ref,
    turned, first_in, proj_ref,
):
    count = x_ref.shape[0] // SLOT
    step = pl.program_id(0)

    @pl.when(step == 0)
    def _():
        turned[...] = normed_ref[...].T
        first_in[...] = jnp.zeros_like(first_in)

    grid_ref[...] = jnp.zeros_like(grid_ref)

    def one_sequence(s, carry):
        rows = pl.ds(pl.multiple_of(s * SLOT, SLOT), SLOT)
        query_grad, keys_grad, values_grad, scores_grads = attend_back(
            query_ref[0, rows, :], keys_ref[0, rows, :], values_ref[0, rows, :], low_ref[rows, :],
            [probs_ref[half, s] for half in range(2)],
        )
        small = jnp.where(buckets[s] == 0, 1.0, 0.0)
        for half in range(2):
            grid_ref[0, half] += scores_grads[half] * small
            grid_ref[1, half] += scores_grads[half] * (1.0 - small)
        proj_ref[rows, 0:128] = query_grad
        proj_ref[rows, 128:256] = keys_grad
        proj_ref[rows, 256:384] = values_grad
        return carry

    lax.fori_loop(0, count, one_sequence, 0)
    proj = proj_ref[...]
    weight_grad_ref[0] = nn(turned[...], proj).astype(BF16)
    pair_ref[0] = jnp.broadcast_to(column_sum(proj.astype(F32)), (8, 384))
    weights = jnp.concatenate([weight_q[...], weight_k[...], weight_v[...]], 1)
    first_in[...] += nt(proj, weights)

    @pl.when(step == PAIRS - 1)
    def _():
        sums_ref[...] = jnp.zeros_like(sums_ref)

        def one_block(b, carry):
            rows = pl.ds(pl.multiple_of(b * SLOT, SLOT), SLOT)
            unit, inverse = standardize(x_ref[rows, :].astype(F32))
            grad = first_in[rows, :]
            sums_ref[0:1, :] += column_sum(grad * unit)
            sums_ref[1:2, :] += column_sum(grad)
            back = norm_back(grad * vec_ref[0:1, :], unit, inverse)
            input_grad_ref[rows, :] = (middle_ref[rows, :] + back).astype(BF16)
            return carry

        lax.fori_loop(0, count, one_block, 0)


def attention_back(buckets, probs, qkv, attended_low, normed, tokens, middle_grad, weight, vecs):
    rows = tokens.shape[0]
    count = rows // SLOT

    def whole(shape):
        return pl.BlockSpec(shape, lambda i: (0,) * len(shape), pipeline_mode=pl.Buffered(1))

    def held(shape):
        return pl.BlockSpec(shape, lambda i: (0,) * len(shape))

    def panel(base):
        return pl.BlockSpec((1, rows, 128), lambda i: (base + i, 0, 0))

    def weight_panel(base):
        return pl.BlockSpec((D, 128), lambda i: (0, base + i))

    return pl.pallas_call(
        attention_back_kernel,
        grid=(PAIRS,),
        in_specs=[
            pl.BlockSpec(memory_space=pltpu.SMEM),
            pl.BlockSpec((2, count, SLOT, SLOT), lambda i: (i, 0, 0, 0)),
            panel(0), panel(PAIRS), panel(2 * PAIRS),
            pl.BlockSpec((rows, 128), lambda i: (0, i)),
            whole((rows, D)), whole((rows, D)), whole((rows, D)),
            weight_panel(0), weight_panel(PAIRS), weight_panel(2 * PAIRS),
            whole((8, D)),
        ],
        out_specs=[
            held((rows, D)),
            pl.BlockSpec((2, 2, SLOT, SLOT), lambda i: (0, i, 0, 0)),
            pl.BlockSpec((1, D, 384), lambda i: (i, 0, 0)),
            pl.BlockSpec((1, 8, 384), lambda i: (i, 0, 0)),
            held((8, D)),
        ],
        out_shape=[
            jax.ShapeDtypeStruct((rows, D), BF16),
            jax.ShapeDtypeStruct((2, HEADS, SLOT, SLOT), F32),
            jax.ShapeDtypeStruct((PAIRS, D, 384), BF16),
            jax.ShapeDtypeStruct((PAIRS, 8, 384), F32),
            jax.ShapeDtypeStruct((8, D), F32),
        ],
        scratch_shapes=[
            pltpu.VMEM((D, rows), BF16),
            pltpu.VMEM((rows, D), F32),
            pltpu.VMEM((rows, 384), BF16),
        ],
        compiler_params=params(dimension_semantics=("arbitrary",)),
        name="attention_backward",
    )(buckets, probs, qkv, qkv, qkv, attended_low, normed, tokens, middle_grad, weight, weight, weight, vecs)


MESH = pl.DeviceIdType.MESH
ANY = pl.ANY


class Place:
    def __init__(self):
        fsdp = lax.axis_index("fsdp")
        dp = lax.axis_index("dp")
        self.z, self.y, self.x, self.core = fsdp // 2, fsdp % 2, dp // 2, dp % 2

    def at(self, z=None, y=None, x=None, core=None):
        z = self.z if z is None else z
        y = self.y if y is None else y
        x = self.x if x is None else x
        core = self.core if core is None else core
        return (z * 2 + y, x * 2 + core)

    def greet(self):
        barrier = pltpu.get_barrier_semaphore()
        peers = [self.at(z=(self.z + k) % 4, y=self.y) for k in range(1, 4)]
        peers += [self.at(z=(self.z + k) % 4, y=1 - self.y) for k in range(4)]
        peers += [
            self.at(x=1 - self.x),
            self.at(core=1 - self.core),
            self.at(x=1 - self.x, core=1 - self.core),
        ]
        for peer in peers:
            pl.semaphore_signal(barrier, inc=1, device_id=peer, device_id_type=MESH)

    def meet(self):
        pl.semaphore_wait(pltpu.get_barrier_semaphore(), 10)


def remote(src, dst, send, recv, peer):
    return pltpu.make_async_remote_copy(
        src_ref=src, dst_ref=dst, send_sem=send, recv_sem=recv, device_id=peer, device_id_type=MESH
    )


def rows_of(first, size):
    return pl.ds(pl.multiple_of(first * size, size), size)


def chunk(kind, ref, r, d):
    if kind == "panel":
        return ref.at[d, rows_of(r, 96), :]
    if kind == "wide":
        return ref.at[rows_of(r, 96), rows_of(d, 768)]
    return ref.at[rows_of(d, 192), rows_of(r, 384)]


class Gather:
    def __init__(self, place, pieces, fulls, send, recv, local):
        self.place, self.pieces, self.fulls = place, pieces, fulls
        self.send, self.recv, self.local = send, recv, local
        self.made = {}

    def slot(self, w, z, y, x):
        return chunk(GATHER_KINDS[w], self.fulls[w], z * 2 + y, x * 2 + self.place.core)

    def copy(self, w, index, src, dst, peer):
        self.made[w, index] = remote(src, dst, self.send.at[w, index], self.recv.at[w, index], peer)
        return self.made[w, index]

    def sources(self, w, k):
        here = self.place
        over_x = (k + GATHER_TURN[w]) % 2 == 0
        near = (here.y, 1 - here.x) if over_x else (1 - here.y, here.x)
        far = (1 - here.y, here.x) if over_x else (here.y, 1 - here.x)
        upper = here.z // 2
        depth = here.z + upper * (3 - 2 * here.z)
        z = k - depth if k == 1 else k
        z = z + upper * (3 - 2 * z) if k else here.z
        return z, near, far

    def plan(self, w):
        here = self.place
        own = self.slot(w, here.z, here.y, here.x)
        self.made[w, "keep"] = pltpu.make_async_copy(self.pieces[w], own, self.local.at[w])
        sibling = here.at(core=1 - here.core)
        pair = here.at(z=here.z + 1 - 2 * (here.z % 2))
        across = here.at(z=3 - here.z)
        for k in range(4):
            z, near, far = self.sources(w, k)
            mine = self.slot(w, z, here.y, here.x)
            src = mine if k else self.pieces[w]
            if k == 0:
                self.copy(w, 1, src, mine, pair)
                self.copy(w, 2, src, mine, across)
            elif k == 1:
                self.copy(w, 3, src, mine, across)
            else:
                self.made[w, "on", k] = remote(
                    src, mine, self.send.at[w, 30 + k], self.recv.at[w, k], pair
                )
            self.copy(w, 4 + k, src, mine, here.at(y=near[0], x=near[1]))
            passed = self.slot(w, z, *near)
            self.copy(w, 8 + 2 * k, src, mine, here.at(y=far[0], x=far[1]))
            self.copy(w, 9 + 2 * k, passed, passed, here.at(y=far[0], x=far[1]))
            third = self.slot(w, z, *far)
            fourth = self.slot(w, z, 1 - here.y, 1 - here.x)
            for n, part in enumerate((src, passed, third, fourth)):
                dst = mine if n == 0 else part
                self.copy(w, 16 + 4 * k + n, part, dst, sibling)

    def when_middle(self, act):
        pl.when(self.place.z * (3 - self.place.z) > 0)(act)

    def begin(self, w):
        self.made[w, "keep"].start()
        self.made[w, 1].start()
        self.when_middle(lambda: self.made[w, 2].start())

    def first(self, w, k):
        if k:
            self.made[w, k].wait_recv()
            on = self.made[w, 3] if k == 1 else self.made[w, "on", k]
            self.when_middle(lambda: on.start())
        self.made[w, 4 + k].start()
        self.made[w, 16 + 4 * k].start()

    def second(self, w, k):
        self.made[w, 4 + k].wait_recv()
        self.made[w, 8 + 2 * k].start()
        self.made[w, 9 + 2 * k].start()
        self.made[w, 17 + 4 * k].start()

    def third(self, w, k):
        for n in range(2):
            self.made[w, 8 + 2 * k + n].wait_recv()
            self.made[w, 18 + 4 * k + n].start()

    def finish(self, w):
        for n in range(16):
            self.made[w, 16 + n].wait_recv()
        for n in [1] + list(range(4, 32)):
            self.made[w, n].wait_send()

        def passed_on():
            for made in (self.made[w, 2], self.made[w, 3], self.made[w, "on", 2], self.made[w, "on", 3]):
                made.wait_send()

        self.when_middle(passed_on)
        self.made[w, "keep"].wait()


MIXED, UP, DOWN = range(3)
GATHER_TURN = (0, 1, 0)
GATHER_KINDS = ("wide", "wide", "turned")


def lined(ref, row, width):
    return jnp.concatenate([ref[f, row : row + 1, :width].astype(F32) for f in range(8)], 1)


def forward_kernel(
    lengths, buckets, x_ref, cot_ref, qkv_p, out_p, up_p, down_t, table_p, head_scale, *refs,
):
    vectors = refs[:12]
    (
    normed_ref, qkv_ref, probs_ref, result_ref, mixed_ref, second_ref, act_ref, low_ref, branch_ref,
    middle_grad_ref, attended_low_ref, sums_ref, wide_sums_ref, vec_ref, qkv_out,
    mixed_p, scale_ref, vec_wide, vec_p, qkv_w, up_w, down_w, vec_f, out_w, bias_ref, wide_ref, qkv_bias_ref, table_ref,
    wall_small, wall_large, visual, attended_ref, gelu_ref, slope_ref, grad_ref,
    send, recv, local, small_send, small_recv, small_local, qkv_sem,
    ) = refs[12:]
    step = pl.program_id(0)
    count = pl.num_programs(0) // 2
    place = Place()
    gather = Gather(place, (mixed_p, up_p, down_t), (qkv_w, up_w, down_w), send, recv, local)
    for w in range(3):
        gather.plan(w)
    f = place.z * 2 + place.y
    small = [pltpu.make_async_copy(vec_p, vec_f.at[f], small_local)]
    for k in range(1, 8):
        peer = (f + k) % 8
        small.append(
            remote(
                vec_p, vec_f.at[f], small_send.at[k], small_recv.at[k],
                place.at(z=peer // 2, y=peer % 2),
            )
        )
    keep_qkv = pltpu.make_async_copy(qkv_w, qkv_out, qkv_sem)

    @pl.when(step == 0)
    def _():
        place.greet()
        vec_wide[...] = jnp.zeros_like(vec_wide)
        for n, vector in enumerate(vectors):
            size = vector.shape[0]
            vec_wide[n : n + 1, :size] = vector[...].astype(F32).reshape(1, size)
        vec_wide[16 : 16 + HEADS, :192] = table_p[...].astype(F32)
        vec_wide[12:13, :HEADS] = head_scale[...].astype(F32).reshape(1, HEADS)
        vec_p[...] = vec_wide[...].astype(BF16)
        head = lax.broadcasted_iota(jnp.int32, (128, D), 0)
        spread = (head == lax.broadcasted_iota(jnp.int32, (128, D), 1) // HEAD_DIM).astype(F32)
        scale_ref[...] = nn(vec_p[...], jnp.concatenate([spread, jnp.zeros((256, D), F32)], 0).astype(BF16))[8:16]
        mixed_p[:, :576] = qkv_p[...]
        mixed_p[:, 576:] = out_p[...]
        place.meet()
        for made in small:
            made.start()
        gather.begin(MIXED)
        gather.first(MIXED, 0)
        gather.first(UP, 0)
        gather.first(DOWN, 0)
        for made in small:
            made.wait()
        for n in range(8):
            vec_ref[n : n + 1, :] = lined(vec_f, n, 96)
        for n in range(3):
            wide_ref[n : n + 1, :] = lined(vec_f, 8 + n, 384)
        pair = lined(vec_f, 11, 192)
        qkv_bias_ref[0:1, :] = jnp.concatenate([pair[:, :D], jnp.zeros((1, D), F32), pair[:, D:]], 1)
        lane = lax.broadcasted_iota(jnp.int32, (1, 3 * D), 1)
        qkv_bias_ref[1:2, :] = jnp.where(lane < D, HEAD_DIM ** (-0.5), 1.0)
        table_ref[...] = jnp.concatenate([vec_f[n, 16:32, :192].astype(F32) for n in range(8)], 1)
        bias_walls(table_ref, wall_small, wall_large, visual)
        heads = functools.partial(bias_head, table_ref, bias_ref, wall_small, wall_large, visual)
        gather.first(MIXED, 1)
        gather.begin(UP)
        gather.second(MIXED, 0)
        gather.second(UP, 0)
        gather.first(MIXED, 2)
        gather.second(DOWN, 0)
        lax.fori_loop(0, 2, heads, 0)
        gather.first(MIXED, 3)
        gather.begin(DOWN)
        gather.second(MIXED, 1)
        gather.third(MIXED, 0)
        lax.fori_loop(2, 4, heads, 0)
        gather.second(MIXED, 2)
        gather.first(UP, 1)
        gather.third(UP, 0)
        lax.fori_loop(4, 6, heads, 0)
        gather.second(MIXED, 3)
        gather.third(DOWN, 0)
        gather.third(MIXED, 1)
        gather.first(UP, 2)
        lax.fori_loop(6, 8, heads, 0)
        gather.second(UP, 1)
        gather.first(UP, 3)
        gather.third(MIXED, 2)
        gather.first(DOWN, 1)
        lax.fori_loop(8, HEADS, heads, 0)
        gather.second(UP, 2)
        gather.third(MIXED, 3)
        gather.finish(MIXED)
        keep_qkv.start()
        sums_ref[...] = jnp.zeros_like(sums_ref)
        wide_sums_ref[...] = jnp.zeros_like(wide_sums_ref)

    schedule = [
        [("first", DOWN, 2)],
        [("second", UP, 3)],
        [("third", UP, 1), ("first", DOWN, 3)],
        [("second", DOWN, 1)],
        [("third", UP, 2)],
        [("second", DOWN, 2)],
        [("third", UP, 3)],
        [("second", DOWN, 3)],
        [("third", DOWN, 1)],
        [],
        [("third", DOWN, 2)],
        [],
    ]

    def progress(spot):
        for s in range(count):
            todo = schedule[3 * s + spot]
            if todo:

                @pl.when(step == s)
                def _(todo=todo):
                    for name, w, k in todo:
                        getattr(gather, name)(w, k)

    @pl.when(step < count)
    def _():
        rows = pl.ds(pl.multiple_of(step * SLOT, SLOT), SLOT)
        progress(0)
        unit, inverse = standardize(x_ref[...].astype(F32))
        normed = (unit * vec_ref[0:1, :] + vec_ref[1:2, :]).astype(BF16)
        normed_ref[...] = normed
        for d in range(4):
            cols = slice(576 * d, 576 * d + 576)
            out = (nn(normed, qkv_w[:, 768 * d : 768 * d + 576]) + qkv_bias_ref[0:1, cols]) * qkv_bias_ref[1:2, cols]
            qkv_ref[:, cols] = out.astype(BF16)
        live = lax.broadcasted_iota(jnp.int32, (SLOT, SLOT), 1) < lengths[step]
        bucket = buckets[step]
        for pair in range(PAIRS):
            if pair % 3 == 0:
                progress(1 + pair // 3)
            query = qkv_ref[:, 128 * pair : 128 * pair + 128]
            keys = qkv_ref[:, D + 128 * pair : D + 128 * pair + 128]
            values = qkv_ref[:, 2 * D + 128 * pair : 2 * D + 128 * pair + 128]
            bias = [bias_ref[bucket, 2 * pair + half] for half in range(2)]
            probs, out = attend(query, keys, values, bias, live)
            for half in range(2):
                probs_ref[2 * pair + half, 0] = probs[half]
            attended_ref[rows, 128 * pair : 128 * pair + 128] = out

    @pl.when(step == count)
    def _():
        gather.finish(UP)
        gather.third(DOWN, 3)
        for d in range(4):
            out_w[:, 192 * d : 192 * d + 192] = qkv_w[:, 768 * d + 576 : 768 * d + 768]

    @pl.when(step >= count)
    def _():
        rows = pl.ds(pl.multiple_of((step - count) * SLOT, SLOT), SLOT)

        def wait_down():
            @pl.when(step == count)
            def _():
                gather.finish(DOWN)

        feed_block(
            x_ref, attended_ref.at[rows, :], cot_ref, out_w, up_w, down_w, vec_ref, wide_ref,
            scale_ref.at[4:5, :],
            result_ref, mixed_ref, second_ref, act_ref, low_ref, branch_ref, middle_grad_ref,
            attended_low_ref, sums_ref, wide_sums_ref, gelu_ref, slope_ref, grad_ref, wait_down,
        )

    @pl.when(step == 2 * count - 1)
    def _():
        keep_qkv.wait()


def forward(lengths, buckets, tokens, cotangent, qkv_p, out_p, up_p, down_p, table_p, head_scale, vectors):
    rows = tokens.shape[0]
    count = rows // SLOT
    smem = pl.BlockSpec(memory_space=pltpu.SMEM)

    def early(shape):
        return pl.BlockSpec(shape, lambda i: (jnp.minimum(i, count - 1),) + (0,) * (len(shape) - 1))

    def late(shape):
        return pl.BlockSpec(shape, lambda i: (jnp.maximum(i - count, 0),) + (0,) * (len(shape) - 1))

    def held(shape):
        return pl.BlockSpec(shape, lambda i: (0,) * len(shape))

    block = (SLOT, D)
    wide = (SLOT, FF)
    return pl.pallas_call(
        forward_kernel,
        grid=(2 * count,),
        in_specs=[
            smem, smem, pl.BlockSpec(block, lambda i: (i % count, 0)), late(block),
            held((96, 576)), held((96, 192)), pl.BlockSpec(memory_space=ANY),
            pl.BlockSpec(memory_space=ANY), held((HEADS, 192)), held((HEADS,)),
        ]
        + [held(vector.shape) for vector in vectors],
        out_specs=[
            early(block), early((SLOT, 3 * D)),
            pl.BlockSpec((HEADS, 1, SLOT, SLOT), lambda i: (0, jnp.minimum(i, count - 1), 0, 0)),
            late(block), late(block), late(block), late(wide), late(wide), late(block), late(block),
            late(block), held((16, D)), held((8, FF)), held((8, D)), pl.BlockSpec(memory_space=ANY),
        ],
        out_shape=[
            jax.ShapeDtypeStruct((rows, D), BF16),
            jax.ShapeDtypeStruct((rows, 3 * D), BF16),
            jax.ShapeDtypeStruct((HEADS, count, SLOT, SLOT), BF16),
            jax.ShapeDtypeStruct((rows, D), BF16),
            jax.ShapeDtypeStruct((rows, D), BF16),
            jax.ShapeDtypeStruct((rows, D), BF16),
            jax.ShapeDtypeStruct((rows, FF), BF16),
            jax.ShapeDtypeStruct((rows, FF), BF16),
            jax.ShapeDtypeStruct((rows, D), BF16),
            jax.ShapeDtypeStruct((rows, D), F32),
            jax.ShapeDtypeStruct((rows, D), BF16),
            jax.ShapeDtypeStruct((16, D), F32),
            jax.ShapeDtypeStruct((8, FF), F32),
            jax.ShapeDtypeStruct((8, D), F32),
            jax.ShapeDtypeStruct((D, FF), BF16),
        ],
        scratch_shapes=[
            pltpu.VMEM((96, D), BF16),
            pltpu.VMEM((8, D), F32),
            pltpu.VMEM((32, 384), F32),
            pltpu.VMEM((32, 384), BF16),
            pltpu.VMEM((D, FF), BF16),
            pltpu.VMEM((D, FF), BF16),
            pltpu.VMEM((D, FF), BF16),
            pltpu.VMEM((8, 32, 384), BF16),
            pltpu.VMEM((D, D), BF16),
            pltpu.VMEM((2, HEADS, SLOT, SLOT), BF16),
            pltpu.VMEM((8, FF), F32),
            pltpu.VMEM((8, 3 * D), F32),
            pltpu.VMEM((16, TABLE), F32),
            pltpu.VMEM((2, 128, 128), F32),
            pltpu.VMEM((4, 256, 128), F32),
            pltpu.VMEM((SLOT, SLOT), F32),
            pltpu.VMEM((rows, D), F32),
            pltpu.VMEM(wide, F32),
            pltpu.VMEM(wide, F32),
            pltpu.VMEM(wide, F32),
            pltpu.SemaphoreType.DMA((3, 34)),
            pltpu.SemaphoreType.DMA((3, 32)),
            pltpu.SemaphoreType.DMA((3,)),
            pltpu.SemaphoreType.DMA((8,)),
            pltpu.SemaphoreType.DMA((8,)),
            pltpu.SemaphoreType.DMA,
            pltpu.SemaphoreType.DMA,
        ],
        compiler_params=params(
            collective_id=1, has_side_effects=True, dimension_semantics=("arbitrary",)
        ),
        name="forward",
    )(lengths, buckets, tokens, cotangent, qkv_p, out_p, up_p, down_p, table_p, head_scale, *vectors)


ORDER = (1, 2, 3, 0)


class Scatter:
    def __init__(self, place, kind, grad, out, buffers):
        self.place, self.kind, self.grad, self.out = place, kind, grad, out
        self.cores, self.over_x, self.over_y, self.far, self.quarter, self.send, self.recv = buffers
        self.made = {}
        here = place
        for k in range(4):
            z = (here.z + k) % 4
            mine = 2 * here.x + here.core
            other = 2 * (1 - here.x) + here.core
            for x in range(2):
                self.copy(
                    k, x, self.block(2 * x + 1 - here.core, z), self.from_core(k, x),
                    here.at(core=1 - here.core),
                )
            if k % 2 == 0:
                self.copy(k, 2, self.block(other, z), self.over_x.at[k // 2], here.at(x=1 - here.x))
                self.copy(
                    k, 4, self.part(mine, z, 1 - here.y), self.far.at[k], here.at(y=1 - here.y)
                )
            else:
                for x in range(2):
                    self.copy(
                        k, 2 + x, self.part(2 * x + here.core, z, 1 - here.y),
                        self.over_y.at[k // 2, x], here.at(y=1 - here.y),
                    )
                self.copy(k, 4, self.part(other, z, here.y), self.far.at[k], here.at(x=1 - here.x))
            if k:
                self.copy(k, 5, self.part(mine, z, here.y), self.quarter.at[k - 1], here.at(z=z))

    def from_core(self, k, x):
        return self.cores.at[k, x, :, : self.over_x.shape[-1]]

    def block(self, d, z):
        if self.kind == "panel":
            return self.grad.at[d, rows_of(z, 192), :]
        if self.kind == "wide":
            return self.grad.at[rows_of(z, 192), rows_of(d, 768)]
        return self.grad.at[rows_of(d, 192), rows_of(z, 768)]

    def part(self, d, z, y):
        if self.kind == "panel":
            return self.grad.at[d, rows_of(2 * z + y, 96), :]
        if self.kind == "wide":
            return self.grad.at[rows_of(2 * z + y, 96), rows_of(d, 768)]
        return self.grad.at[rows_of(d, 192), rows_of(2 * z + y, 384)]

    def copy(self, k, index, src, dst, peer):
        self.made[k, index] = remote(src, dst, self.send.at[k, index], self.recv.at[k, index], peer)

    def add(self, target, source):
        def some(n, carry):
            at = rows_of(n, 16)
            target[at, :] = target[at, :] + source[at, :]
            return carry

        lax.fori_loop(0, target.shape[0] // 16, some, 0)

    def core(self, k):
        for x in range(2):
            self.made[k, x].start()

    def plane(self, k):
        here = self.place
        z = (here.z + k) % 4
        for x in range(2):
            self.made[k, x].wait_recv()
            self.add(self.block(2 * x + here.core, z), self.from_core(k, x))
        self.made[k, 2].start()
        if k % 2:
            self.made[k, 3].start()

    def turn(self, k):
        here = self.place
        z = (here.z + k) % 4
        self.made[k, 2].wait_recv()
        if k % 2 == 0:
            self.add(self.block(2 * here.x + here.core, z), self.over_x.at[k // 2])
        else:
            self.made[k, 3].wait_recv()
            for x in range(2):
                self.add(self.part(2 * x + here.core, z, here.y), self.over_y.at[k // 2, x])
        self.made[k, 4].start()

    def line(self, k):
        here = self.place
        self.made[k, 4].wait_recv()
        self.add(self.part(2 * here.x + here.core, (here.z + k) % 4, here.y), self.far.at[k])
        if k:
            self.made[k, 5].start()

    def end(self):
        here = self.place
        for k in range(1, 4):
            self.made[k, 5].wait_recv()
        total = self.part(2 * here.x + here.core, here.z, here.y)[...].astype(F32)
        for k in range(3):
            total = total + self.quarter[k].astype(F32)
        self.out[...] = total[:, : self.out.shape[1]]
        for made in self.made.values():
            made.wait_send()


def scatter_scratch(kind, width):
    half = (192, width // 2) if kind == "turned" else (96, width)
    return [
        pltpu.VMEM((4, 2, 192, width), BF16),
        pltpu.VMEM((2, 192, width), BF16),
        pltpu.VMEM((2, 2) + half, BF16),
        pltpu.VMEM((4,) + half, BF16),
        pltpu.VMEM((3,) + half, BF16),
        pltpu.SemaphoreType.DMA((4, 6)),
        pltpu.SemaphoreType.DMA((4, 6)),
    ]


def pack_sums(sums_ref, first_ref, wide_ref, pair, table_ref, packed):
    low = first_ref[0:2, :]
    narrow = sums_ref[...]
    group = lax.broadcasted_iota(jnp.int32, (D, 128), 0) // HEAD_DIM
    pick = (group == lax.broadcasted_iota(jnp.int32, (D, 128), 1)).astype(F32).astype(BF16)
    high, rest = split_low(narrow[8:16])
    heads = (nn(high, pick) + nn(rest, pick))[0:1]
    heads = jnp.concatenate([heads, jnp.zeros((1, 64), F32)], 1)
    for f in range(8):
        at = slice(96 * f, 96 * f + 96)
        packed[f, 0:1, :] = jnp.concatenate(
            [low[0:1, at], low[1:2, at], narrow[2:3, at], narrow[3:4, at]], 1
        )
        packed[f, 1:2, :] = jnp.concatenate([narrow[n : n + 1, at] for n in range(4, 8)], 1)
        packed[f, 2:5, :] = wide_ref[0:3, 384 * f : 384 * f + 384]
        at = slice(192 * f, 192 * f + 192)
        packed[f, 5:6, :] = jnp.concatenate([pair[:, at], heads], 1)
        for n in range(PAIRS):
            packed[f, 6 + n : 7 + n, :] = jnp.concatenate(
                [table_ref[2 * n : 2 * n + 1, at], table_ref[2 * n + 1 : 2 * n + 2, at]], 1
            )
        packed[f, 12:16, :] = jnp.zeros((4, 384), F32)


class SmallSums:
    def __init__(self, place, packed, rows, peers, sems):
        self.place, self.packed, self.rows, self.peers = place, packed, rows, peers
        self.send, self.recv = sems

    def begin(self):
        here = self.place
        f = here.z * 2 + here.y
        self.made = []
        for k in range(1, 8):
            to = (f + k) % 8
            made = remote(
                self.packed.at[to], self.rows.at[k - 1], self.send.at[k], self.recv.at[k],
                here.at(z=to // 2, y=to % 2),
            )
            made.start()
            self.made.append(made)

    def cross(self):
        here = self.place
        f = here.z * 2 + here.y
        for made in self.made:
            made.wait()
        total = self.packed[f]
        for k in range(7):
            total = total + self.rows[k]
        self.peers[0] = total
        d = here.x * 2 + here.core
        self.made = []
        for k in range(1, 4):
            to = (d + k) % 4
            made = remote(
                self.peers.at[0], self.peers.at[k], self.send.at[7 + k], self.recv.at[7 + k],
                here.at(x=to // 2, core=to % 2),
            )
            made.start()
            self.made.append(made)

    def end(self):
        for made in self.made:
            made.wait()
        return (self.peers[0] + self.peers[1]) + (self.peers[2] + self.peers[3])


BACK_SCHEDULE = {
    3: [("down", "plane", 0)],
    4: [("down", "plane", 1)],
    5: [("down", "plane", 2)],
    6: [("down", "plane", 3)],
    7: [("down", "turn", 0)],
    8: [("down", "turn", 1)],
    10: [("down", "turn", 2), ("up", "plane", 0)],
    11: [("down", "line", 1), ("down", "turn", 3), ("up", "plane", 1), ("up", "plane", 2)],
    12: [("up", "plane", 3), ("out", "plane", 0), ("out", "plane", 1), ("out", "plane", 2), ("out", "plane", 3)],
    13: [("down", "line", 0)],
    14: [("down", "line", 2)],
    15: [("up", "turn", 0)],
    17: [("down", "line", 3)],
    18: [("up", "turn", 1)],
    22: [("up", "turn", 2), ("qkv", "plane", 0)],
    23: [("up", "turn", 3), ("out", "turn", 0), ("qkv", "plane", 1), ("qkv", "plane", 2)],
    24: [("out", "turn", 1), ("out", "turn", 2), ("qkv", "plane", 3)],
    25: [("out", "turn", 3)],
}
BACK_DRAIN = [
    ("up", "line", 1),
    ("up", "line", 0),
    ("up", "line", 2),
    ("qkv", "turn", 0),
    ("out", "line", 0),
    ("up", "line", 3),
    ("qkv", "turn", 1),
    ("out", "line", 2),
    ("qkv", "turn", 2),
    ("out", "line", 1),
    ("out", "line", 3),
    ("qkv", "turn", 3),
    ("qkv", "line", 1),
    ("qkv", "line", 0),
    ("qkv", "line", 3),
    ("qkv", "line", 2),
]


def backward_kernel(
    buckets, cot_hbm, act_ref, second_hbm, low_ref, mixed_hbm, branch_hbm, normed_hbm,
    probs_ref, query_ref, keys_ref, values_ref, attended_low_ref, vec_ref, sums_ref, wide_ref,
    x_hbm, middle_hbm, weight_hbm,
    input_grad_ref, down_out, up_out, out_out, qkv_out, total_ref,
    left, turned, middle_ref, first_in, proj, grid_ref, down_ref, up_ref, out_ref, qkv_ref,
    table_ref, first_ref, wall_small, wall_large, packed, gathered, peers, small_send, small_recv,
    loading, middle_sem, *buffers,
):
    step = pl.program_id(0)
    place = Place()
    parts = {
        "down": Scatter(place, "turned", down_ref, down_out, buffers[0:7]),
        "up": Scatter(place, "wide", up_ref, up_out, buffers[7:14]),
        "out": Scatter(place, "panel", out_ref, out_out, buffers[14:21]),
        "qkv": Scatter(place, "panel", qkv_ref, qkv_out, buffers[0:1] + buffers[21:27]),
    }
    small = SmallSums(place, packed, gathered, peers, (small_send, small_recv))
    count = query_ref.shape[0] // SLOT

    def load(n, src, dst):
        return pltpu.make_async_copy(src, dst, loading.at[n])

    load_cot = load(0, cot_hbm, left.at[0])
    load_second = load(1, second_hbm, left.at[1])
    load_mixed = load(2, mixed_hbm, left.at[0])
    load_branch = load(3, branch_hbm, left.at[1])
    load_normed = load(4, normed_hbm, left.at[0])
    load_x = load(5, x_hbm, left.at[1])

    def load_middle(b):
        n = b % 2
        return pltpu.make_async_copy(middle_hbm.at[rows_of(b, SLOT), :], middle_ref.at[n], middle_sem.at[n])

    load_weight = load(7, weight_hbm, down_ref)

    def progress(at):
        for name, event, n in BACK_SCHEDULE.get(at, []):
            getattr(parts[name], event)(ORDER[n])

    def down_panel():
        z = (place.z + 1 + step) % 4
        down_ref[:, rows_of(z, 768)] = nn(turned[...], act_ref[...]).astype(BF16)

    @pl.when(step == 0)
    def _():
        place.greet()
        load_cot.start()
        load_second.start()
        place.meet()

    for at in BACK_SCHEDULE:
        if at < 23:
            pl.when(step == at)(functools.partial(progress, at))

    @pl.when(step < 4)
    def _():
        @pl.when(step == 0)
        def _():
            load_cot.wait()
            turned[...] = left[0].T
            load_mixed.start()

        down_panel()
        for n in range(4):
            pl.when(step == n)(functools.partial(parts["down"].core, ORDER[n]))

    @pl.when((step >= 4) & (step < 8))
    def _():
        @pl.when(step == 4)
        def _():
            load_second.wait()
            turned[...] = left[1].T
            load_branch.start()

        up_ref[:, rows_of(step - 4, 768)] = nn(turned[...], low_ref[...]).astype(BF16)

        @pl.when(step == 7)
        def _():
            for k in ORDER:
                parts["up"].core(k)

    @pl.when(step == 8)
    def _():
        load_mixed.wait()
        turned[...] = left[0].T
        load_normed.start()
        load_branch.wait()
        for d in range(4):
            out_ref[d] = nn(turned[...], left[1, :, 192 * d : 192 * d + 192]).astype(BF16)
        for k in ORDER:
            parts["out"].core(k)
        load_x.start()
        table_grad_start(table_ref, wall_small, wall_large)

    @pl.when((step >= 9) & (step < 15))
    def _():
        pair = step - 9
        cols = rows_of(pair, 128)
        for s in range(count):
            rows = slice(s * SLOT, s * SLOT + SLOT)
            query_grad, keys_grad, values_grad, scores_grads = attend_back(
                query_ref[rows, :], keys_ref[rows, :], values_ref[rows, :], attended_low_ref[rows, :],
                [probs_ref[half, s] for half in range(2)],
            )
            proj[0, rows, cols] = query_grad
            proj[1, rows, cols] = keys_grad
            proj[2, rows, cols] = values_grad
            chosen = jnp.where(buckets[s] == 0, 1.0, 0.0)
            for half in range(2):
                if s == 0:
                    grid_ref[0, half] = scores_grads[half] * chosen
                    grid_ref[1, half] = scores_grads[half] * (1.0 - chosen)
                else:
                    grid_ref[0, half] += scores_grads[half] * chosen
                    grid_ref[1, half] += scores_grads[half] * (1.0 - chosen)
        for half in range(2):
            table_grad_head(grid_ref, table_ref, wall_small, wall_large, 2 * pair + half, half)

    def lay_panel(d):
        def lay(pieces):
            at = 0
            for n, first, last in pieces:
                left[0, :, at : at + last - first] = proj[n, :, first:last]
                at += last - first

        cuts = (
            [(0, 0, 576)], [(0, 576, 768), (1, 0, 384)], [(1, 384, 768), (2, 0, 192)], [(2, 192, 768)],
        )
        for n, pieces in enumerate(cuts):
            pl.when(d == n)(functools.partial(lay, pieces))

    @pl.when((step >= 15) & (step < 19))
    def _():
        @pl.when(step == 15)
        def _():
            load_normed.wait()
            turned[...] = left[0].T

        lay_panel(step - 15)
        grad = nn(turned[...], left[0, :, :576]).astype(BF16)
        qkv_ref[step - 15] = jnp.concatenate([grad, jnp.zeros((D, 64), BF16)], 1)

        @pl.when(step == 18)
        def _():
            for k in ORDER:
                parts["qkv"].core(k)

    @pl.when(step == 19)
    def _():
        parts["down"].end()
        load_weight.start()

    @pl.when((step >= 19) & (step < 23))
    def _():
        lay_panel(step - 19)

        @pl.when(step == 19)
        def _():
            load_weight.wait()
            first_in[...] = jnp.zeros_like(first_in)

        first_in[...] += nt(left[0, :, :576], down_ref[:, pl.ds(pl.multiple_of(768 * (step - 19), 768), 576)])

    @pl.when(step == 23)
    def _():
        progress(23)
        load_middle(0).start()
        load_x.wait()
        first_ref[...] = jnp.zeros_like(first_ref)

        def one_block(b, carry):
            rows = pl.ds(pl.multiple_of(b * SLOT, SLOT), SLOT)
            unit, inverse = standardize(left[1, rows, :].astype(F32))
            grad = first_in[rows, :]
            first_ref[0:1, :] += column_sum(grad * unit)
            first_ref[1:2, :] += column_sum(grad)
            back = norm_back(grad * vec_ref[0:1, :], unit, inverse)

            @pl.when(b + 1 < count)
            def _():
                load_middle(b + 1).start()

            load_middle(b).wait()
            input_grad_ref[rows, :] = (middle_ref[b % 2] + back).astype(BF16)
            return carry

        lax.fori_loop(0, count, one_block, 0)
        progress(24)
        table_grad_end(table_ref, wall_small, wall_large)
        pair = jnp.concatenate([tall_sum(proj.at[0]), tall_sum(proj.at[2])], 1)
        progress(25)
        pack_sums(sums_ref, first_ref, wide_ref, pair, table_ref, packed)
        small.begin()
        for n, (name, event, k) in enumerate(BACK_DRAIN):
            if n == len(BACK_DRAIN) // 2:
                small.cross()
            getattr(parts[name], event)(ORDER[k])
        parts["up"].end()
        parts["out"].end()
        total_ref[...] = small.end()
        parts["qkv"].end()


def backward(
    buckets, cotangent, act, second, low, mixed, branch, normed, probs, qkv, attended_low, vecs,
    sums, wide, tokens, middle_grad, weight,
):
    rows = cotangent.shape[0]
    count = rows // SLOT
    any_space = pl.BlockSpec(memory_space=ANY)

    def held(shape):
        return pl.BlockSpec(shape, lambda i: (0,) * len(shape))

    def pair(i):
        return jnp.clip(i - 9, 0, PAIRS - 1)

    def panel(base):
        return pl.BlockSpec((rows, 128), lambda i: (0, base + pair(i)))

    def act_panel(i):
        return (0, (lax.axis_index("fsdp") // 2 + 1 + jnp.minimum(i, 3)) % 4)

    outs = [(192, 384), (96, 768), (96, 192), (96, 576), (16, 384)]
    return pl.pallas_call(
        backward_kernel,
        grid=(24,),
        in_specs=[
            pl.BlockSpec(memory_space=pltpu.SMEM),
            any_space,
            pl.BlockSpec((rows, D), act_panel),
            any_space,
            pl.BlockSpec((rows, D), lambda i: (0, jnp.clip(i - 4, 0, 3))),
            any_space, any_space, any_space,
            pl.BlockSpec((2, count, SLOT, SLOT), lambda i: (pair(i), 0, 0, 0)),
            panel(0), panel(PAIRS), panel(2 * PAIRS), panel(0),
            held((8, D)), held((16, D)), held((8, FF)),
            any_space, any_space, any_space,
        ],
        out_specs=[held((rows, D))] + [held(shape) for shape in outs],
        out_shape=[jax.ShapeDtypeStruct((rows, D), BF16)]
        + [jax.ShapeDtypeStruct(shape, F32) for shape in outs],
        scratch_shapes=[
            pltpu.VMEM((2, rows, D), BF16),
            pltpu.VMEM((D, rows), BF16),
            pltpu.VMEM((2, SLOT, D), F32),
            pltpu.VMEM((rows, D), F32),
            pltpu.VMEM((3, rows, D), BF16),
            pltpu.VMEM((2, 2, SLOT, SLOT), F32),
            pltpu.VMEM((D, FF), BF16),
            pltpu.VMEM((D, FF), BF16),
            pltpu.VMEM((4, D, 192), BF16),
            pltpu.VMEM((4, D, 640), BF16),
            pltpu.VMEM((16, TABLE), F32),
            pltpu.VMEM((8, D), F32),
            pltpu.VMEM((2, 128, 128), F32),
            pltpu.VMEM((4, 256, 128), F32),
            pltpu.VMEM((8, 16, 384), F32),
            pltpu.VMEM((7, 16, 384), F32),
            pltpu.VMEM((4, 16, 384), F32),
            pltpu.SemaphoreType.DMA((11,)),
            pltpu.SemaphoreType.DMA((11,)),
            pltpu.SemaphoreType.DMA((8,)),
            pltpu.SemaphoreType.DMA((2,)),
        ]
        + scatter_scratch("turned", 768) + scatter_scratch("wide", 768)
        + scatter_scratch("panel", 192) + scatter_scratch("panel", 640)[1:],
        compiler_params=pltpu.CompilerParams(
            collective_id=2, has_side_effects=True, dimension_semantics=("arbitrary",),
            vmem_limit_bytes=BACK_LIMIT,
        ),
        name="backward",
    )(
        buckets, cotangent, act, second, low, mixed, branch, normed, probs, qkv, qkv, qkv,
        attended_low, vecs, sums, wide, tokens, middle_grad, weight,
    )


def emit_kernel(count, total_ref, *refs):
    sources = refs[:count]
    targets = refs[count : 2 * count]
    small = refs[2 * count : 2 * count + 14]
    held = refs[2 * count + 14 : -2]
    into, out = refs[-2:]
    loads = [
        pltpu.make_async_copy(src, dst, into.at[n]) for n, (src, dst) in enumerate(zip(sources, held))
    ]
    made = [
        pltpu.make_async_copy(src, dst, out.at[n]) for n, (src, dst) in enumerate(zip(held, targets))
    ]
    for each in loads:
        each.start()
    for load, each in zip(loads, made):
        load.wait()
        each.start()
    total = total_ref[...]
    for n in range(8):
        at = 96 * (n % 4)
        small[n][...] = total[n // 4 : n // 4 + 1, at : at + 96].reshape(96)
    for n in range(3):
        small[8 + n][...] = total[2 + n : 3 + n, :].reshape(384)
    small[11][...] = total[5:6, 0:192].reshape(192)
    small[12][...] = total[5:6, 192:204].reshape(HEADS)
    for n in range(PAIRS):
        small[13][2 * n : 2 * n + 1, :] = total[6 + n : 7 + n, 0:192]
        small[13][2 * n + 1 : 2 * n + 2, :] = total[6 + n : 7 + n, 192:384]
    for each in made:
        each.wait()


def emit(total, *large):
    vmem = pl.BlockSpec(memory_space=pltpu.VMEM)
    any_space = pl.BlockSpec(memory_space=ANY)
    small = [(96,)] * 8 + [(384,)] * 3 + [(192,), (HEADS,), (HEADS, 192)]
    return pl.pallas_call(
        functools.partial(emit_kernel, len(large)),
        in_specs=[vmem] + [any_space] * len(large),
        out_specs=[any_space] * len(large) + [vmem] * len(small),
        out_shape=[jax.ShapeDtypeStruct(part.shape, part.dtype) for part in large]
        + [jax.ShapeDtypeStruct(shape, F32) for shape in small],
        scratch_shapes=[pltpu.VMEM(part.shape, part.dtype) for part in large]
        + [pltpu.SemaphoreType.DMA((len(large),))] * 2,
        compiler_params=params(),
        name="emit",
    )(total, *large)


def gather_matrix(piece):
    rows = lax.all_gather(piece, "fsdp", axis=0, tiled=True)
    return lax.all_gather(rows, "dp", axis=1, tiled=True)


def scatter_matrix(grad):
    part = lax.psum_scatter(grad, "dp", scatter_dimension=1, tiled=True).astype(F32)
    return lax.psum_scatter(part, "fsdp", scatter_dimension=0, tiled=True)


def body(
    tokens, cotangent, lengths, buckets, qkv_weight, query_value_bias, out_weight, out_bias,
    up_weight, up_bias, down_weight, down_bias, first_gain, first_shift, mix_gain, mix_shift,
    second_gain, second_shift, hidden_gain, hidden_shift, head_scale, position_table,
):
    parts = lax.axis_size("fsdp")
    own_kernels = (parts, lax.axis_size("dp")) == (8, 4)
    narrow = [
        first_gain, first_shift, mix_gain, mix_shift, second_gain, second_shift, out_bias, down_bias,
    ]
    wide = [up_bias, hidden_gain, hidden_shift]
    a = D // parts
    b = FF // parts
    if own_kernels:
        (
            normed, qkv, probs, result, mixed, second, act, low, branch, middle_grad, attended_low,
            sums, wide_sums, vecs, qkv_full,
        ) = forward(
            lengths, buckets, tokens, cotangent, qkv_weight, out_weight, up_weight, down_weight.T,
            position_table.T, head_scale, narrow + wide + [query_value_bias],
        )
        input_grad, down_owned, up_owned, out_owned, qkv_owned, total = backward(
            buckets, cotangent, act, second, low, mixed, branch, normed, probs, qkv, attended_low,
            vecs, sums, wide_sums, tokens, middle_grad, qkv_full,
        )
        result, input_grad, qkv_owned, out_owned, up_owned, down_owned, *small = emit(
            total, result, input_grad, qkv_owned, out_owned, up_owned, down_owned
        )
        down_owned = down_owned.T
        narrow_owned = small[:8]
        wide_owned = small[8:11]
        pair_owned, scale_grad, table_owned = small[11], small[12], small[13].T
    else:
        packed = jnp.concatenate(
            [jnp.pad(jnp.stack(narrow), ((0, 0), (0, b - a))), jnp.stack(wide)]
            + [jnp.pad(query_value_bias, (0, b - 2 * a))[None], jnp.zeros((4, b), BF16)]
            + [jnp.pad(position_table.T, ((0, 4), (0, b - 2 * a)))]
        )
        scales = jnp.repeat(head_scale.astype(F32), HEAD_DIM)[None]
        gathered = lax.all_gather(packed, "fsdp", axis=0)
        qkv_full = gather_matrix(qkv_weight)
        out_full = gather_matrix(out_weight)
        up_full = gather_matrix(up_weight)
        down_full = gather_matrix(down_weight).T
        gathered = gathered.astype(F32)
        vecs = gathered[:, :8, :a].transpose(1, 0, 2).reshape(8, D)
        wides = jnp.pad(gathered[:, 8:11].transpose(1, 0, 2).reshape(3, FF), ((0, 5), (0, 0)))
        pair = gathered[:, 11, : 2 * a].reshape(1, 2 * D)
        table = gathered[:, 16:, : 2 * a].transpose(1, 0, 2).reshape(16, TABLE)
        qkv_bias = jnp.concatenate([pair[:, :D], jnp.zeros((1, D), F32), pair[:, D:]], 1)

        bias = build_bias(table)
        normed, qkv, probs, attended = attention(
            lengths, buckets, tokens, vecs, qkv_full, qkv_bias, bias
        )
        (
            result, mixed, second, act, low, branch, middle_grad, attended_low, sums, wide_sums,
        ) = feed_forward(tokens, attended, cotangent, out_full, up_full, down_full, vecs, wides, scales)
        down_grad = outer_product(cotangent, act, 512)
        up_grad = outer_product(second, low, 512)
        out_grad = outer_product(mixed, branch, 256)
        input_grad, grids, qkv_grad, pair_sums, first_sums = attention_back(
            buckets, probs, qkv, attended_low, normed, tokens, middle_grad, qkv_full, vecs
        )
        table_sums = table_grad(grids)
        qkv_natural = qkv_grad.reshape(PAIRS, D, 3, 128).transpose(1, 2, 0, 3).reshape(D, 3 * D)

        qkv_owned = scatter_matrix(qkv_natural)
        out_owned = scatter_matrix(out_grad)
        up_owned = scatter_matrix(up_grad)
        down_owned = scatter_matrix(down_grad.T)
        pair_grad = pair_sums[:, 0].reshape(PAIRS, 3, 128).transpose(1, 0, 2).reshape(3, D)
        pair_grad = jnp.concatenate([pair_grad[0], pair_grad[2]])
        narrow_sums = jnp.concatenate([first_sums[:2], sums[2:8]], 0)
        packed = jnp.concatenate(
            [
                narrow_sums.reshape(8, parts, a).transpose(1, 0, 2).reshape(parts, -1),
                wide_sums[:3].reshape(3, parts, b).transpose(1, 0, 2).reshape(parts, -1),
                pair_grad.reshape(parts, -1),
                table_sums[:HEADS].T.reshape(parts, -1),
            ],
            1,
        )
        owned = lax.psum(lax.psum_scatter(packed, "fsdp", scatter_dimension=0, tiled=True), "dp")[0]
        scale_grad = lax.psum(sums[8].reshape(HEADS, HEAD_DIM).sum(1), ("fsdp", "dp"))
        narrow_owned = owned[: 8 * a].reshape(8, a)
        edge = 8 * a
        wide_owned = owned[edge : edge + 3 * b].reshape(3, b)
        edge += 3 * b
        pair_owned = owned[edge : edge + 2 * a]
        edge += 2 * a
        table_owned = owned[edge:].reshape(TABLE // parts, HEADS)
    return (
        result, input_grad, qkv_owned, pair_owned, out_owned, narrow_owned[6], up_owned,
        wide_owned[0], down_owned, narrow_owned[7], narrow_owned[0], narrow_owned[1],
        narrow_owned[2], narrow_owned[3], narrow_owned[4], narrow_owned[5], wide_owned[1],
        wide_owned[2], scale_grad, table_owned,
    )


def solution(mesh):
    tokens = P(("fsdp", "dp"), None)
    sequences = P(("fsdp", "dp"))
    matrix = P("fsdp", "dp")
    vector = P("fsdp")
    table = P("fsdp", None)
    in_specs = (
        tokens, tokens, sequences, sequences, matrix, vector, matrix, vector, matrix, vector,
        matrix, vector, vector, vector, vector, vector, vector, vector, vector, vector, P(), table,
    )
    out_specs = (
        tokens, tokens, matrix, vector, matrix, vector, matrix, vector, matrix, vector, vector,
        vector, vector, vector, vector, vector, vector, vector, P(), table,
    )
    return jax.shard_map(body, mesh=mesh, in_specs=in_specs, out_specs=out_specs, check_vma=False)
```

profile of v0, /device:TPU:0, one launch (start us, length us, event | category | flops | bytes accessed | tf_op | source)
XLA Modules:
  0.0 235.4 jit_solution(5075042405664257451)
XLA Ops:
  0.7 123.8 %forward.1 = (bf16[1024,768]{1,0:T(8,128)(2,1)}, bf16[1024,2304]{1,0:T(8,128)(2,1)}, bf16[12,4,256,256]{3,2,1,0:T(8,128)(2,1)}, bf16[1024,768]{1,0:T(8,128)(2,1)...) custom-call(s32[4]{0:T(128)} %lengths.1, ...), custom_call_target="tpu_custom_call" | custom-call | tf_op jit(solution)/shard_map/forward/pallas_call | solution.py:919
  124.5 105.9 %backward.1 = (bf16[1024,768]{1,0:T(8,128)(2,1)}, f32[192,384]{1,0:T(8,128)}, f32[96,768]{1,0:T(8,128)}, f32[96,192]{1,0:T(8,128)}, f32[96,576]{1,0:T(8,128)}, /*index=5*/f32[16,384]{1,0:T(8,128)}) custom-call(s32[4]{0:T(128)} %buckets.3, bf16[1024,768]{1,0:T(8,128)(2,1)} %cot_hbm.1, bf16[1024,3072]{1,0:T(8,128)(2,1)} %get-tuple-element.61.act_ref, ...), custom_call_target="tpu_custom_call" | custom-call | tf_op jit(solution)/shard_map/backward/pallas_call | solution.py:1439
  230.4 4.9 %emit.1 = (bf16[1024,768]{1,0:T(8,128)(2,1)}, bf16[1024,768]{1,0:T(8,128)(2,1)}, f32[96,576]{1,0:T(8,128)}, f32[96,192]{1,0:T(8,128)}, f32[96,768]{1,0:T(8,128)}...) custom-call(f32[16,384]{1,0:T(8,128)} %get-tuple-element.75.total_re, ...), custom_call_target="tpu_custom_call" | custom-call | tf_op jit(solution)/shard_map/emit/pallas_call | solution.py:1529
where the time goes:
time: 236 us; the launch traced here: 235 us
  Pallas kernels  235 us (100%)
    pallas_call x1, Pallas kernels, forward(): pl.pallas_call(forward_kernel, grid=(2 * count,), in_specs=[smem, smem, p...  124 us
    pallas_call x1, Pallas kernels, backward(): pl.pallas_call(backward_kernel, grid=(24,), in_specs=[pl.BlockSpec(memory...  106 us
    pallas_call x1, Pallas kernels, emit(): pl.pallas_call(functools.partial(emit_kernel, len(large)), in_specs=[vmem...  4.89 us

commit v1 on v0

--- a/solution.py
+++ b/solution.py
@@ -678,16 +678,21 @@
     def when_middle(self, act):
         pl.when(self.place.z * (3 - self.place.z) > 0)(act)
 
-    def begin(self, w):
+    def begin(self, w, k=0):
         self.made[w, "keep"].start()
         self.made[w, 1].start()
         self.when_middle(lambda: self.made[w, 2].start())
 
+    def relay(self, w, k):
+        def on():
+            self.made[w, k].wait_recv()
+            (self.made[w, 3] if k == 1 else self.made[w, "on", k]).start()
+
+        self.when_middle(on)
+
     def first(self, w, k):
         if k:
-            self.made[w, k].wait_recv()
-            on = self.made[w, 3] if k == 1 else self.made[w, "on", k]
-            self.when_middle(lambda: on.start())
+            pl.when(self.place.z * (3 - self.place.z) == 0)(self.made[w, k].wait_recv)
         self.made[w, 4 + k].start()
         self.made[w, 16 + 4 * k].start()
 
@@ -719,6 +724,55 @@
 MIXED, UP, DOWN = range(3)
 GATHER_TURN = (0, 1, 0)
 GATHER_KINDS = ("wide", "wide", "turned")
+
+
+GATHER_SCHEDULE = [
+    [("begin", MIXED, 0), ("first", MIXED, 0), ("first", UP, 0)],
+    [("first", DOWN, 0)],
+    [("begin", DOWN, 0)],
+    [],
+    [],
+    [("second", MIXED, 0), ("relay", MIXED, 1), ("first", MIXED, 1), ("relay", MIXED, 2), ("second", UP, 0)],
+    [
+        ("begin", UP, 0),
+        ("relay", DOWN, 1),
+        ("first", DOWN, 1),
+        ("first", MIXED, 2),
+        ("relay", MIXED, 3),
+        ("relay", UP, 1),
+        ("third", MIXED, 0),
+        ("first", UP, 1),
+        ("relay", UP, 2),
+        ("second", MIXED, 1),
+        ("first", MIXED, 3),
+        ("second", MIXED, 2),
+        ("relay", DOWN, 3),
+        ("first", UP, 2),
+        ("second", UP, 1),
+        ("relay", UP, 3),
+        ("second", MIXED, 3),
+        ("first", DOWN, 3),
+        ("first", UP, 3),
+        ("third", MIXED, 1),
+        ("third", MIXED, 2),
+        ("second", UP, 2),
+        ("third", MIXED, 3),
+    ],
+    [],
+    [],
+    [("third", UP, 1)],
+    [("second", UP, 3), ("relay", DOWN, 2), ("second", DOWN, 1)],
+    [],
+    [("third", UP, 0), ("third", UP, 2), ("second", DOWN, 0)],
+    [],
+    [("first", DOWN, 2)],
+    [],
+    [("third", UP, 3), ("second", DOWN, 3)],
+    [("third", DOWN, 1)],
+    [],
+    [("second", DOWN, 2)],
+    [("third", DOWN, 0), ("third", DOWN, 3), ("third", DOWN, 2)],
+]
 
 
 def lined(ref, row, width):
@@ -754,6 +808,10 @@
         )
     keep_qkv = pltpu.make_async_copy(qkv_w, qkv_out, qkv_sem)
 
+    def follow(point):
+        for name, w, k in GATHER_SCHEDULE[point]:
+            getattr(gather, name)(w, k)
+
     @pl.when(step == 0)
     def _():
         place.greet()
@@ -772,10 +830,7 @@
         place.meet()
         for made in small:
             made.start()
-        gather.begin(MIXED)
-        gather.first(MIXED, 0)
-        gather.first(UP, 0)
-        gather.first(DOWN, 0)
+        follow(0)
         for made in small:
             made.wait()
         for n in range(8):
@@ -789,63 +844,19 @@
         table_ref[...] = jnp.concatenate([vec_f[n, 16:32, :192].astype(F32) for n in range(8)], 1)
         bias_walls(table_ref, wall_small, wall_large, visual)
         heads = functools.partial(bias_head, table_ref, bias_ref, wall_small, wall_large, visual)
-        gather.first(MIXED, 1)
-        gather.begin(UP)
-        gather.second(MIXED, 0)
-        gather.second(UP, 0)
-        gather.first(MIXED, 2)
-        gather.second(DOWN, 0)
-        lax.fori_loop(0, 2, heads, 0)
-        gather.first(MIXED, 3)
-        gather.begin(DOWN)
-        gather.second(MIXED, 1)
-        gather.third(MIXED, 0)
-        lax.fori_loop(2, 4, heads, 0)
-        gather.second(MIXED, 2)
-        gather.first(UP, 1)
-        gather.third(UP, 0)
-        lax.fori_loop(4, 6, heads, 0)
-        gather.second(MIXED, 3)
-        gather.third(DOWN, 0)
-        gather.third(MIXED, 1)
-        gather.first(UP, 2)
-        lax.fori_loop(6, 8, heads, 0)
-        gather.second(UP, 1)
-        gather.first(UP, 3)
-        gather.third(MIXED, 2)
-        gather.first(DOWN, 1)
-        lax.fori_loop(8, HEADS, heads, 0)
-        gather.second(UP, 2)
-        gather.third(MIXED, 3)
+        for n, last in enumerate((2, 4, 6, 9, HEADS)):
+            follow(1 + n)
+            lax.fori_loop((0, 2, 4, 6, 9)[n], last, heads, 0)
+        follow(6)
         gather.finish(MIXED)
         keep_qkv.start()
         sums_ref[...] = jnp.zeros_like(sums_ref)
         wide_sums_ref[...] = jnp.zeros_like(wide_sums_ref)
 
-    schedule = [
-        [("first", DOWN, 2)],
-        [("second", UP, 3)],
-        [("third", UP, 1), ("first", DOWN, 3)],
-        [("second", DOWN, 1)],
-        [("third", UP, 2)],
-        [("second", DOWN, 2)],
-        [("third", UP, 3)],
-        [("second", DOWN, 3)],
-        [("third", DOWN, 1)],
-        [],
-        [("third", DOWN, 2)],
-        [],
-    ]
-
     def progress(spot):
         for s in range(count):
-            todo = schedule[3 * s + spot]
-            if todo:
-
-                @pl.when(step == s)
-                def _(todo=todo):
-                    for name, w, k in todo:
-                        getattr(gather, name)(w, k)
+            if GATHER_SCHEDULE[7 + 3 * s + spot]:
+                pl.when(step == s)(functools.partial(follow, 7 + 3 * s + spot))
 
     @pl.when(step < count)
     def _():
@@ -874,8 +885,8 @@
 
     @pl.when(step == count)
     def _():
+        follow(7 + 3 * count)
         gather.finish(UP)
-        gather.third(DOWN, 3)
         for d in range(4):
             out_w[:, 192 * d : 192 * d + 192] = qkv_w[:, 768 * d + 576 : 768 * d + 768]
 
@@ -886,6 +897,7 @@
         def wait_down():
             @pl.when(step == count)
             def _():
+                follow(8 + 3 * count)
                 gather.finish(DOWN)
 
         feed_block(
@@ -1173,36 +1185,34 @@
 
 BACK_SCHEDULE = {
     3: [("down", "plane", 0)],
-    4: [("down", "plane", 1)],
-    5: [("down", "plane", 2)],
-    6: [("down", "plane", 3)],
-    7: [("down", "turn", 0)],
-    8: [("down", "turn", 1)],
-    10: [("down", "turn", 2), ("up", "plane", 0)],
-    11: [("down", "line", 1), ("down", "turn", 3), ("up", "plane", 1), ("up", "plane", 2)],
-    12: [("up", "plane", 3), ("out", "plane", 0), ("out", "plane", 1), ("out", "plane", 2), ("out", "plane", 3)],
-    13: [("down", "line", 0)],
-    14: [("down", "line", 2)],
-    15: [("up", "turn", 0)],
-    17: [("down", "line", 3)],
-    18: [("up", "turn", 1)],
-    22: [("up", "turn", 2), ("qkv", "plane", 0)],
-    23: [("up", "turn", 3), ("out", "turn", 0), ("qkv", "plane", 1), ("qkv", "plane", 2)],
-    24: [("out", "turn", 1), ("out", "turn", 2), ("qkv", "plane", 3)],
-    25: [("out", "turn", 3)],
+    4: [("down", "plane", 1), ("down", "plane", 2)],
+    5: [("down", "plane", 3)],
+    6: [("down", "turn", 0)],
+    7: [("down", "turn", 1)],
+    8: [("down", "turn", 2)],
+    10: [("down", "turn", 3), ("down", "line", 1), ("up", "plane", 0), ("up", "plane", 1), ("up", "plane", 2)],
+    11: [
+        ("down", "line", 0),
+        ("up", "plane", 3),
+        ("out", "plane", 0),
+        ("out", "plane", 1),
+        ("out", "plane", 2),
+        ("down", "line", 2),
+        ("out", "plane", 3),
+    ],
+    12: [("down", "line", 3)],
+    14: [("up", "turn", 0), ("up", "turn", 1)],
+    16: [("up", "turn", 2), ("up", "turn", 3)],
+    17: [("out", "turn", 0), ("out", "turn", 1), ("out", "turn", 3)],
+    18: [("up", "line", 0), ("out", "turn", 2), ("up", "line", 1)],
+    19: [("up", "line", 2), ("up", "line", 3), ("out", "line", 0)],
+    20: [("out", "line", 1), ("out", "line", 2), ("out", "line", 3), ("qkv", "plane", 0), ("qkv", "plane", 1)],
+    21: [("qkv", "plane", 2), ("qkv", "plane", 3)],
 }
 BACK_DRAIN = [
-    ("up", "line", 1),
-    ("up", "line", 0),
-    ("up", "line", 2),
     ("qkv", "turn", 0),
-    ("out", "line", 0),
-    ("up", "line", 3),
     ("qkv", "turn", 1),
-    ("out", "line", 2),
     ("qkv", "turn", 2),
-    ("out", "line", 1),
-    ("out", "line", 3),
     ("qkv", "turn", 3),
     ("qkv", "line", 1),
     ("qkv", "line", 0),
@@ -1263,7 +1273,7 @@
         place.meet()
 
     for at in BACK_SCHEDULE:
-        if at < 23:
+        if at < 19:
             pl.when(step == at)(functools.partial(progress, at))
 
     @pl.when(step < 4)
@@ -1347,37 +1357,31 @@
     def _():
         @pl.when(step == 15)
         def _():
+            parts["down"].end()
+            load_weight.start()
             load_normed.wait()
             turned[...] = left[0].T
-
-        lay_panel(step - 15)
+            first_in[...] = jnp.zeros_like(first_in)
+
+        d = step - 15
+        lay_panel(d)
         grad = nn(turned[...], left[0, :, :576]).astype(BF16)
-        qkv_ref[step - 15] = jnp.concatenate([grad, jnp.zeros((D, 64), BF16)], 1)
+        qkv_ref[d] = jnp.concatenate([grad, jnp.zeros((D, 64), BF16)], 1)
+
+        @pl.when(step == 15)
+        def _():
+            load_weight.wait()
 
         @pl.when(step == 18)
         def _():
             for k in ORDER:
                 parts["qkv"].core(k)
 
+        first_in[...] += nt(left[0, :, :576], down_ref[:, pl.ds(pl.multiple_of(768 * d, 768), 576)])
+
     @pl.when(step == 19)
     def _():
-        parts["down"].end()
-        load_weight.start()
-
-    @pl.when((step >= 19) & (step < 23))
-    def _():
-        lay_panel(step - 19)
-
-        @pl.when(step == 19)
-        def _():
-            load_weight.wait()
-            first_in[...] = jnp.zeros_like(first_in)
-
-        first_in[...] += nt(left[0, :, :576], down_ref[:, pl.ds(pl.multiple_of(768 * (step - 19), 768), 576)])
-
-    @pl.when(step == 23)
-    def _():
-        progress(23)
+        progress(19)
         load_middle(0).start()
         load_x.wait()
         first_ref[...] = jnp.zeros_like(first_ref)
@@ -1399,10 +1403,10 @@
             return carry
 
         lax.fori_loop(0, count, one_block, 0)
-        progress(24)
+        progress(20)
         table_grad_end(table_ref, wall_small, wall_large)
         pair = jnp.concatenate([tall_sum(proj.at[0]), tall_sum(proj.at[2])], 1)
-        progress(25)
+        progress(21)
         pack_sums(sums_ref, first_ref, wide_ref, pair, table_ref, packed)
         small.begin()
         for n, (name, event, k) in enumerate(BACK_DRAIN):
@@ -1438,7 +1442,7 @@
     outs = [(192, 384), (96, 768), (96, 192), (96, 576), (16, 384)]
     return pl.pallas_call(
         backward_kernel,
-        grid=(24,),
+        grid=(20,),
         in_specs=[
             pl.BlockSpec(memory_space=pltpu.SMEM),
             any_space,

time: 236 us -> 226 us (0.958)
  Pallas kernels: 235 us -> 225 us
    pallas_call x1, Pallas kernels: 124 us -> 118 us  [forward(): pl.pallas_call(forward_kernel, grid=(2 * count,), in_specs=[smem, smem, p...]
    pallas_call x1, Pallas kernels: 106 us -> 102 us  [backward(): pl.pallas_call(backward_kernel, grid=(20,), in_specs=[pl.BlockSpec(memory...]
where the time goes in v1:
time: 226 us
  Pallas kernels  225 us (100%)
    pallas_call x1, Pallas kernels, forward(): pl.pallas_call(forward_kernel, grid=(2 * count,), in_specs=[smem, smem, p...  118 us
    pallas_call x1, Pallas kernels, backward(): pl.pallas_call(backward_kernel, grid=(20,), in_specs=[pl.BlockSpec(memory...  102 us
    pallas_call x1, Pallas kernels, emit(): pl.pallas_call(functools.partial(emit_kernel, len(large)), in_specs=[vmem...  4.89 us

profile of v1, /device:TPU:0, one launch (start us, length us, event | category | flops | bytes accessed | tf_op | source)
XLA Modules:
  0.0 225.9 jit_solution(2984019022343923573)
XLA Ops:
  0.7 117.8 %forward.1 = (bf16[1024,768]{1,0:T(8,128)(2,1)}, bf16[1024,2304]{1,0:T(8,128)(2,1)}, bf16[12,4,256,256]{3,2,1,0:T(8,128)(2,1)}, bf16[1024,768]{1,0:T(8,128)(2,1)...) custom-call(s32[4]{0:T(128)} %lengths.1, ...), custom_call_target="tpu_custom_call" | custom-call | tf_op jit(solution)/shard_map/forward/pallas_call | solution.py:931
  118.4 102.4 %backward.1 = (bf16[1024,768]{1,0:T(8,128)(2,1)}, f32[192,384]{1,0:T(8,128)}, f32[96,768]{1,0:T(8,128)}, f32[96,192]{1,0:T(8,128)}, f32[96,576]{1,0:T(8,128)}, /*index=5*/f32[16,384]{1,0:T(8,128)}) custom-call(s32[4]{0:T(128)} %buckets.3, bf16[1024,768]{1,0:T(8,128)(2,1)} %cot_hbm.1, bf16[1024,3072]{1,0:T(8,128)(2,1)} %get-tuple-element.61.act_ref, ...), custom_call_target="tpu_custom_call" | custom-call | tf_op jit(solution)/shard_map/backward/pallas_call | solution.py:1443
  220.9 4.9 %emit.1 = (bf16[1024,768]{1,0:T(8,128)(2,1)}, bf16[1024,768]{1,0:T(8,128)(2,1)}, f32[96,576]{1,0:T(8,128)}, f32[96,192]{1,0:T(8,128)}, f32[96,768]{1,0:T(8,128)}...) custom-call(f32[16,384]{1,0:T(8,128)} %get-tuple-element.75.total_re, ...), custom_call_target="tpu_custom_call" | custom-call | tf_op jit(solution)/shard_map/emit/pallas_call | solution.py:1533

commit v2 on v1

--- a/solution.py
+++ b/solution.py
@@ -1000,8 +1000,9 @@
 
 
 class Scatter:
-    def __init__(self, place, kind, grad, out, buffers):
+    def __init__(self, place, kind, grad, out, buffers, flip=0, offset=0):
         self.place, self.kind, self.grad, self.out = place, kind, grad, out
+        self.flip, self.offset = flip, offset
         self.cores, self.over_x, self.over_y, self.far, self.quarter, self.send, self.recv = buffers
         self.made = {}
         here = place
@@ -1014,7 +1015,7 @@
                     k, x, self.block(2 * x + 1 - here.core, z), self.from_core(k, x),
                     here.at(core=1 - here.core),
                 )
-            if k % 2 == 0:
+            if self.x_first(k):
                 self.copy(k, 2, self.block(other, z), self.over_x.at[k // 2], here.at(x=1 - here.x))
                 self.copy(
                     k, 4, self.part(mine, z, 1 - here.y), self.far.at[k], here.at(y=1 - here.y)
@@ -1029,8 +1030,11 @@
             if k:
                 self.copy(k, 5, self.part(mine, z, here.y), self.quarter.at[k - 1], here.at(z=z))
 
+    def x_first(self, k):
+        return (k + self.flip) % 2 == 0
+
     def from_core(self, k, x):
-        return self.cores.at[k, x, :, : self.over_x.shape[-1]]
+        return self.cores.at[k, x, :, self.offset : self.offset + self.over_x.shape[-1]]
 
     def block(self, d, z):
         if self.kind == "panel":
@@ -1068,14 +1072,14 @@
             self.made[k, x].wait_recv()
             self.add(self.block(2 * x + here.core, z), self.from_core(k, x))
         self.made[k, 2].start()
-        if k % 2:
+        if not self.x_first(k):
             self.made[k, 3].start()
 
     def turn(self, k):
         here = self.place
         z = (here.z + k) % 4
         self.made[k, 2].wait_recv()
-        if k % 2 == 0:
+        if self.x_first(k):
             self.add(self.block(2 * here.x + here.core, z), self.over_x.at[k // 2])
         else:
             self.made[k, 3].wait_recv()
@@ -1185,39 +1189,55 @@
 
 BACK_SCHEDULE = {
     3: [("down", "plane", 0)],
-    4: [("down", "plane", 1), ("down", "plane", 2)],
-    5: [("down", "plane", 3)],
-    6: [("down", "turn", 0)],
+    4: [("down", "plane", 1)],
+    5: [("down", "plane", 2)],
+    6: [("down", "plane", 3), ("down", "turn", 0)],
     7: [("down", "turn", 1)],
-    8: [("down", "turn", 2)],
-    10: [("down", "turn", 3), ("down", "line", 1), ("up", "plane", 0), ("up", "plane", 1), ("up", "plane", 2)],
-    11: [
-        ("down", "line", 0),
-        ("up", "plane", 3),
-        ("out", "plane", 0),
-        ("out", "plane", 1),
-        ("out", "plane", 2),
-        ("down", "line", 2),
-        ("out", "plane", 3),
+    10: [
+        ("up", "plane", 0),
+        ("down", "turn", 3),
+        ("down", "turn", 2),
+        ("down", "line", 1),
+        ("up", "plane", 1),
+        ("up", "plane", 2),
     ],
-    12: [("down", "line", 3)],
-    14: [("up", "turn", 0), ("up", "turn", 1)],
-    16: [("up", "turn", 2), ("up", "turn", 3)],
-    17: [("out", "turn", 0), ("out", "turn", 1), ("out", "turn", 3)],
-    18: [("up", "line", 0), ("out", "turn", 2), ("up", "line", 1)],
-    19: [("up", "line", 2), ("up", "line", 3), ("out", "line", 0)],
-    20: [("out", "line", 1), ("out", "line", 2), ("out", "line", 3), ("qkv", "plane", 0), ("qkv", "plane", 1)],
-    21: [("qkv", "plane", 2), ("qkv", "plane", 3)],
+    11: [("down", "line", 0)],
+    12: [("down", "line", 2)],
+    13: [("up", "turn", 0), ("up", "plane", 3)],
+    14: [("out", "plane", 0), ("out", "plane", 1)],
+    15: [("up", "turn", 1), ("down", "line", 3)],
+    16: [("out", "plane", 3), ("out", "plane", 2), ("up", "line", 0)],
+    17: [("up", "turn", 2)],
+    18: [("up", "turn", 3), ("up", "line", 1)],
+    19: [("out", "turn", 3), ("out", "turn", 2), ("out", "turn", 1), ("out", "turn", 0)],
+    20: [("qkv0", "plane", 2), ("qkv0", "plane", 1), ("up", "line", 2), ("qkv0", "plane", 0)],
+    21: [("qkv1", "plane", 0), ("qkv1", "plane", 1)],
 }
 BACK_DRAIN = [
-    ("qkv", "turn", 0),
-    ("qkv", "turn", 1),
-    ("qkv", "turn", 2),
-    ("qkv", "turn", 3),
-    ("qkv", "line", 1),
-    ("qkv", "line", 0),
-    ("qkv", "line", 3),
-    ("qkv", "line", 2),
+    ("qkv0", "turn", 2),
+    ("qkv0", "turn", 1),
+    ("out", "line", 2),
+    ("out", "line", 3),
+    ("out", "line", 0),
+    ("qkv0", "plane", 3),
+    ("qkv0", "turn", 0),
+    ("qkv0", "line", 2),
+    ("qkv1", "turn", 0),
+    ("out", "line", 1),
+    ("qkv1", "plane", 2),
+    ("qkv1", "turn", 1),
+    ("qkv1", "plane", 3),
+    ("qkv0", "line", 1),
+    ("qkv0", "turn", 3),
+    ("qkv0", "line", 0),
+    ("qkv1", "line", 0),
+    ("qkv1", "turn", 2),
+    ("qkv1", "turn", 3),
+    ("qkv1", "line", 1),
+    ("up", "line", 3),
+    ("qkv0", "line", 3),
+    ("qkv1", "line", 2),
+    ("qkv1", "line", 3),
 ]
 
 
@@ -1226,7 +1246,7 @@
     probs_ref, query_ref, keys_ref, values_ref, attended_low_ref, vec_ref, sums_ref, wide_ref,
     x_hbm, middle_hbm, weight_hbm,
     input_grad_ref, down_out, up_out, out_out, qkv_out, total_ref,
-    left, turned, middle_ref, first_in, proj, grid_ref, down_ref, up_ref, out_ref, qkv_ref,
+    left, turned, middle_ref, first_in, proj, grid_ref, down_ref, up_ref, out_ref, qkv_a, qkv_b,
     table_ref, first_ref, wall_small, wall_large, packed, gathered, peers, small_send, small_recv,
     loading, middle_sem, *buffers,
 ):
@@ -1236,7 +1256,10 @@
         "down": Scatter(place, "turned", down_ref, down_out, buffers[0:7]),
         "up": Scatter(place, "wide", up_ref, up_out, buffers[7:14]),
         "out": Scatter(place, "panel", out_ref, out_out, buffers[14:21]),
-        "qkv": Scatter(place, "panel", qkv_ref, qkv_out, buffers[0:1] + buffers[21:27]),
+        "qkv0": Scatter(place, "panel", qkv_a, qkv_out.at[:, 0:256], buffers[0:1] + buffers[21:27]),
+        "qkv1": Scatter(
+            place, "panel", qkv_b, qkv_out.at[:, 256:576], buffers[0:1] + buffers[27:33], 1, 256
+        ),
     }
     small = SmallSums(place, packed, gathered, peers, (small_send, small_recv))
     count = query_ref.shape[0] // SLOT
@@ -1366,7 +1389,8 @@
         d = step - 15
         lay_panel(d)
         grad = nn(turned[...], left[0, :, :576]).astype(BF16)
-        qkv_ref[d] = jnp.concatenate([grad, jnp.zeros((D, 64), BF16)], 1)
+        qkv_a[d] = grad[:, :256]
+        qkv_b[d] = jnp.concatenate([grad[:, 256:], jnp.zeros((D, 64), BF16)], 1)
 
         @pl.when(step == 15)
         def _():
@@ -1375,7 +1399,8 @@
         @pl.when(step == 18)
         def _():
             for k in ORDER:
-                parts["qkv"].core(k)
+                parts["qkv0"].core(k)
+                parts["qkv1"].core(k)
 
         first_in[...] += nt(left[0, :, :576], down_ref[:, pl.ds(pl.multiple_of(768 * d, 768), 576)])
 
@@ -1416,7 +1441,8 @@
         parts["up"].end()
         parts["out"].end()
         total_ref[...] = small.end()
-        parts["qkv"].end()
+        parts["qkv0"].end()
+        parts["qkv1"].end()
 
 
 def backward(
@@ -1468,7 +1494,8 @@
             pltpu.VMEM((D, FF), BF16),
             pltpu.VMEM((D, FF), BF16),
             pltpu.VMEM((4, D, 192), BF16),
-            pltpu.VMEM((4, D, 640), BF16),
+            pltpu.VMEM((4, D, 256), BF16),
+            pltpu.VMEM((4, D, 384), BF16),
             pltpu.VMEM((16, TABLE), F32),
             pltpu.VMEM((8, D), F32),
             pltpu.VMEM((2, 128, 128), F32),
@@ -1482,7 +1509,8 @@
             pltpu.SemaphoreType.DMA((2,)),
         ]
         + scatter_scratch("turned", 768) + scatter_scratch("wide", 768)
-        + scatter_scratch("panel", 192) + scatter_scratch("panel", 640)[1:],
+        + scatter_scratch("panel", 192) + scatter_scratch("panel", 256)[1:]
+        + scatter_scratch("panel", 384)[1:],
         compiler_params=pltpu.CompilerParams(
             collective_id=2, has_side_effects=True, dimension_semantics=("arbitrary",),
             vmem_limit_bytes=BACK_LIMIT,

time: 226 us -> 220 us (0.973)
  Pallas kernels: 225 us -> 219 us
    pallas_call x1, Pallas kernels: 102 us -> 96 us  [backward(): pl.pallas_call(backward_kernel, grid=(20,), in_specs=[pl.BlockSpec(memory...]
where the time goes in v2:
time: 220 us; the launch traced here: 219 us
  Pallas kernels  219 us (100%)
    pallas_call x1, Pallas kernels, forward(): pl.pallas_call(forward_kernel, grid=(2 * count,), in_specs=[smem, smem, p...  118 us
    pallas_call x1, Pallas kernels, backward(): pl.pallas_call(backward_kernel, grid=(20,), in_specs=[pl.BlockSpec(memory...  96 us
    pallas_call x1, Pallas kernels, emit(): pl.pallas_call(functools.partial(emit_kernel, len(large)), in_specs=[vmem...  4.89 us

profile of v2, /device:TPU:0, one launch (start us, length us, event | category | flops | bytes accessed | tf_op | source)
XLA Modules:
  0.0 219.5 jit_solution(8079089474647359754)
XLA Ops:
  0.7 117.8 %forward.1 = (bf16[1024,768]{1,0:T(8,128)(2,1)}, bf16[1024,2304]{1,0:T(8,128)(2,1)}, bf16[12,4,256,256]{3,2,1,0:T(8,128)(2,1)}, bf16[1024,768]{1,0:T(8,128)(2,1)...) custom-call(s32[4]{0:T(128)} %lengths.1, ...), custom_call_target="tpu_custom_call" | custom-call | tf_op jit(solution)/shard_map/forward/pallas_call | solution.py:931
  118.4 96.0 %backward.1 = (bf16[1024,768]{1,0:T(8,128)(2,1)}, f32[192,384]{1,0:T(8,128)}, f32[96,768]{1,0:T(8,128)}, f32[96,192]{1,0:T(8,128)}, f32[96,576]{1,0:T(8,128)}, /*index=5*/f32[16,384]{1,0:T(8,128)}) custom-call(s32[4]{0:T(128)} %buckets.3, bf16[1024,768]{1,0:T(8,128)(2,1)} %cot_hbm.1, bf16[1024,3072]{1,0:T(8,128)(2,1)} %get-tuple-element.61.act_ref, ...), custom_call_target="tpu_custom_call" | custom-call | tf_op jit(solution)/shard_map/backward/pallas_call | solution.py:1469
  214.4 4.9 %emit.1 = (bf16[1024,768]{1,0:T(8,128)(2,1)}, bf16[1024,768]{1,0:T(8,128)(2,1)}, f32[96,576]{1,0:T(8,128)}, f32[96,192]{1,0:T(8,128)}, f32[96,768]{1,0:T(8,128)}...) custom-call(f32[16,384]{1,0:T(8,128)} %get-tuple-element.75.total_re, ...), custom_call_target="tpu_custom_call" | custom-call | tf_op jit(solution)/shard_map/emit/pallas_call | solution.py:1561

commit v3 on v2

--- a/solution.py
+++ b/solution.py
@@ -726,52 +726,53 @@
 GATHER_KINDS = ("wide", "wide", "turned")
 
 
+BEGIN, RELAY, FIRST, SECOND, THIRD = "begin", "relay", "first", "second", "third"
 GATHER_SCHEDULE = [
-    [("begin", MIXED, 0), ("first", MIXED, 0), ("first", UP, 0)],
-    [("first", DOWN, 0)],
-    [("begin", DOWN, 0)],
+    [(BEGIN, MIXED, 0), (FIRST, MIXED, 0), (FIRST, UP, 0)],
+    [(FIRST, DOWN, 0)],
+    [(BEGIN, DOWN, 0)],
     [],
     [],
-    [("second", MIXED, 0), ("relay", MIXED, 1), ("first", MIXED, 1), ("relay", MIXED, 2), ("second", UP, 0)],
+    [(SECOND, MIXED, 0), (RELAY, MIXED, 1), (FIRST, MIXED, 1), (RELAY, MIXED, 2), (SECOND, UP, 0)],
     [
-        ("begin", UP, 0),
-        ("relay", DOWN, 1),
-        ("first", DOWN, 1),
-        ("first", MIXED, 2),
-        ("relay", MIXED, 3),
-        ("relay", UP, 1),
-        ("third", MIXED, 0),
-        ("first", UP, 1),
-        ("relay", UP, 2),
-        ("second", MIXED, 1),
-        ("first", MIXED, 3),
-        ("second", MIXED, 2),
-        ("relay", DOWN, 3),
-        ("first", UP, 2),
-        ("second", UP, 1),
-        ("relay", UP, 3),
-        ("second", MIXED, 3),
-        ("first", DOWN, 3),
-        ("first", UP, 3),
-        ("third", MIXED, 1),
-        ("third", MIXED, 2),
-        ("second", UP, 2),
-        ("third", MIXED, 3),
+        (BEGIN, UP, 0),
+        (RELAY, DOWN, 1),
+        (FIRST, DOWN, 1),
+        (FIRST, MIXED, 2),
+        (RELAY, MIXED, 3),
+        (RELAY, UP, 1),
+        (THIRD, MIXED, 0),
+        (FIRST, UP, 1),
+        (RELAY, UP, 2),
+        (SECOND, MIXED, 1),
+        (FIRST, MIXED, 3),
+        (SECOND, MIXED, 2),
+        (RELAY, DOWN, 3),
+        (FIRST, UP, 2),
+        (SECOND, UP, 1),
+        (RELAY, UP, 3),
+        (SECOND, MIXED, 3),
+        (FIRST, DOWN, 3),
+        (FIRST, UP, 3),
+        (THIRD, MIXED, 1),
+        (THIRD, MIXED, 2),
+        (SECOND, UP, 2),
+        (THIRD, MIXED, 3),
     ],
     [],
     [],
-    [("third", UP, 1)],
-    [("second", UP, 3), ("relay", DOWN, 2), ("second", DOWN, 1)],
+    [(THIRD, UP, 1)],
+    [(SECOND, UP, 3), (RELAY, DOWN, 2), (SECOND, DOWN, 1)],
     [],
-    [("third", UP, 0), ("third", UP, 2), ("second", DOWN, 0)],
+    [(THIRD, UP, 0), (THIRD, UP, 2), (SECOND, DOWN, 0)],
     [],
-    [("first", DOWN, 2)],
+    [(FIRST, DOWN, 2)],
     [],
-    [("third", UP, 3), ("second", DOWN, 3)],
-    [("third", DOWN, 1)],
+    [(THIRD, UP, 3), (SECOND, DOWN, 3)],
+    [(THIRD, DOWN, 1)],
     [],
-    [("second", DOWN, 2)],
-    [("third", DOWN, 0), ("third", DOWN, 3), ("third", DOWN, 2)],
+    [(SECOND, DOWN, 2)],
+    [(THIRD, DOWN, 0), (THIRD, DOWN, 3), (THIRD, DOWN, 2)],
 ]
 
 
@@ -1187,57 +1188,59 @@
         return (self.peers[0] + self.peers[1]) + (self.peers[2] + self.peers[3])
 
 
+GRAD_DOWN, GRAD_UP, GRAD_OUT, GRAD_QKV_A, GRAD_QKV_B = range(5)
+PLANE, TURN, LINE = "plane", "turn", "line"
 BACK_SCHEDULE = {
-    3: [("down", "plane", 0)],
-    4: [("down", "plane", 1)],
-    5: [("down", "plane", 2)],
-    6: [("down", "plane", 3), ("down", "turn", 0)],
-    7: [("down", "turn", 1)],
+    3: [(GRAD_DOWN, PLANE, 0)],
+    4: [(GRAD_DOWN, PLANE, 1)],
+    5: [(GRAD_DOWN, PLANE, 2)],
+    6: [(GRAD_DOWN, PLANE, 3), (GRAD_DOWN, TURN, 0)],
+    7: [(GRAD_DOWN, TURN, 1)],
     10: [
-        ("up", "plane", 0),
-        ("down", "turn", 3),
-        ("down", "turn", 2),
-        ("down", "line", 1),
-        ("up", "plane", 1),
-        ("up", "plane", 2),
+        (GRAD_UP, PLANE, 0),
+        (GRAD_DOWN, TURN, 3),
+        (GRAD_DOWN, TURN, 2),
+        (GRAD_DOWN, LINE, 1),
+        (GRAD_UP, PLANE, 1),
+        (GRAD_UP, PLANE, 2),
     ],
-    11: [("down", "line", 0)],
-    12: [("down", "line", 2)],
-    13: [("up", "turn", 0), ("up", "plane", 3)],
-    14: [("out", "plane", 0), ("out", "plane", 1)],
-    15: [("up", "turn", 1), ("down", "line", 3)],
-    16: [("out", "plane", 3), ("out", "plane", 2), ("up", "line", 0)],
-    17: [("up", "turn", 2)],
-    18: [("up", "turn", 3), ("up", "line", 1)],
-    19: [("out", "turn", 3), ("out", "turn", 2), ("out", "turn", 1), ("out", "turn", 0)],
-    20: [("qkv0", "plane", 2), ("qkv0", "plane", 1), ("up", "line", 2), ("qkv0", "plane", 0)],
-    21: [("qkv1", "plane", 0), ("qkv1", "plane", 1)],
+    11: [(GRAD_DOWN, LINE, 0)],
+    12: [(GRAD_DOWN, LINE, 2)],
+    13: [(GRAD_UP, TURN, 0), (GRAD_UP, PLANE, 3)],
+    14: [(GRAD_OUT, PLANE, 0), (GRAD_OUT, PLANE, 1)],
+    15: [(GRAD_UP, TURN, 1), (GRAD_DOWN, LINE, 3)],
+    16: [(GRAD_OUT, PLANE, 3), (GRAD_OUT, PLANE, 2), (GRAD_UP, LINE, 0)],
+    17: [(GRAD_UP, TURN, 2)],
+    18: [(GRAD_UP, TURN, 3), (GRAD_UP, LINE, 1)],
+    19: [(GRAD_OUT, TURN, 3), (GRAD_OUT, TURN, 2), (GRAD_OUT, TURN, 1), (GRAD_OUT, TURN, 0)],
+    20: [(GRAD_QKV_A, PLANE, 2), (GRAD_QKV_A, PLANE, 1), (GRAD_UP, LINE, 2), (GRAD_QKV_A, PLANE, 0)],
+    21: [(GRAD_QKV_B, PLANE, 0), (GRAD_QKV_B, PLANE, 1)],
 }
 BACK_DRAIN = [
-    ("qkv0", "turn", 2),
-    ("qkv0", "turn", 1),
-    ("out", "line", 2),
-    ("out", "line", 3),
-    ("out", "line", 0),
-    ("qkv0", "plane", 3),
-    ("qkv0", "turn", 0),
-    ("qkv0", "line", 2),
-    ("qkv1", "turn", 0),
-    ("out", "line", 1),
-    ("qkv1", "plane", 2),
-    ("qkv1", "turn", 1),
-    ("qkv1", "plane", 3),
-    ("qkv0", "line", 1),
-    ("qkv0", "turn", 3),
-    ("qkv0", "line", 0),
-    ("qkv1", "line", 0),
-    ("qkv1", "turn", 2),
-    ("qkv1", "turn", 3),
-    ("qkv1", "line", 1),
-    ("up", "line", 3),
-    ("qkv0", "line", 3),
-    ("qkv1", "line", 2),
-    ("qkv1", "line", 3),
+    (GRAD_QKV_A, TURN, 2),
+    (GRAD_QKV_A, TURN, 1),
+    (GRAD_OUT, LINE, 2),
+    (GRAD_OUT, LINE, 3),
+    (GRAD_OUT, LINE, 0),
+    (GRAD_QKV_A, PLANE, 3),
+    (GRAD_QKV_A, TURN, 0),
+    (GRAD_QKV_A, LINE, 2),
+    (GRAD_QKV_B, TURN, 0),
+    (GRAD_OUT, LINE, 1),
+    (GRAD_QKV_B, PLANE, 2),
+    (GRAD_QKV_B, TURN, 1),
+    (GRAD_QKV_B, PLANE, 3),
+    (GRAD_QKV_A, LINE, 1),
+    (GRAD_QKV_A, TURN, 3),
+    (GRAD_QKV_A, LINE, 0),
+    (GRAD_QKV_B, LINE, 0),
+    (GRAD_QKV_B, TURN, 2),
+    (GRAD_QKV_B, TURN, 3),
+    (GRAD_QKV_B, LINE, 1),
+    (GRAD_UP, LINE, 3),
+    (GRAD_QKV_A, LINE, 3),
+    (GRAD_QKV_B, LINE, 2),
+    (GRAD_QKV_B, LINE, 3),
 ]
 
 
@@ -1252,15 +1255,15 @@
 ):
     step = pl.program_id(0)
     place = Place()
-    parts = {
-        "down": Scatter(place, "turned", down_ref, down_out, buffers[0:7]),
-        "up": Scatter(place, "wide", up_ref, up_out, buffers[7:14]),
-        "out": Scatter(place, "panel", out_ref, out_out, buffers[14:21]),
-        "qkv0": Scatter(place, "panel", qkv_a, qkv_out.at[:, 0:256], buffers[0:1] + buffers[21:27]),
-        "qkv1": Scatter(
+    parts = [
+        Scatter(place, "turned", down_ref, down_out, buffers[0:7]),
+        Scatter(place, "wide", up_ref, up_out, buffers[7:14]),
+        Scatter(place, "panel", out_ref, out_out, buffers[14:21]),
+        Scatter(place, "panel", qkv_a, qkv_out.at[:, 0:256], buffers[0:1] + buffers[21:27]),
+        Scatter(
             place, "panel", qkv_b, qkv_out.at[:, 256:576], buffers[0:1] + buffers[27:33], 1, 256
         ),
-    }
+    ]
     small = SmallSums(place, packed, gathered, peers, (small_send, small_recv))
     count = query_ref.shape[0] // SLOT
 
@@ -1309,7 +1312,7 @@
 
         down_panel()
         for n in range(4):
-            pl.when(step == n)(functools.partial(parts["down"].core, ORDER[n]))
+            pl.when(step == n)(functools.partial(parts[GRAD_DOWN].core, ORDER[n]))
 
     @pl.when((step >= 4) & (step < 8))
     def _():
@@ -1324,7 +1327,7 @@
         @pl.when(step == 7)
         def _():
             for k in ORDER:
-                parts["up"].core(k)
+                parts[GRAD_UP].core(k)
 
     @pl.when(step == 8)
     def _():
@@ -1335,7 +1338,7 @@
         for d in range(4):
             out_ref[d] = nn(turned[...], left[1, :, 192 * d : 192 * d + 192]).astype(BF16)
         for k in ORDER:
-            parts["out"].core(k)
+            parts[GRAD_OUT].core(k)
         load_x.start()
         table_grad_start(table_ref, wall_small, wall_large)
 
@@ -1380,7 +1383,7 @@
     def _():
         @pl.when(step == 15)
         def _():
-            parts["down"].end()
+            parts[GRAD_DOWN].end()
             load_weight.start()
             load_normed.wait()
             turned[...] = left[0].T
@@ -1399,8 +1402,8 @@
         @pl.when(step == 18)
         def _():
             for k in ORDER:
-                parts["qkv0"].core(k)
-                parts["qkv1"].core(k)
+                parts[GRAD_QKV_A].core(k)
+                parts[GRAD_QKV_B].core(k)
 
         first_in[...] += nt(left[0, :, :576], down_ref[:, pl.ds(pl.multiple_of(768 * d, 768), 576)])
 
@@ -1438,11 +1441,11 @@
             if n == len(BACK_DRAIN) // 2:
                 small.cross()
             getattr(parts[name], event)(ORDER[k])
-        parts["up"].end()
-        parts["out"].end()
+        parts[GRAD_UP].end()
+        parts[GRAD_OUT].end()
         total_ref[...] = small.end()
-        parts["qkv0"].end()
-        parts["qkv1"].end()
+        parts[GRAD_QKV_A].end()
+        parts[GRAD_QKV_B].end()
 
 
 def backward(

time: 220 us -> 220 us (level)
  no operation moved by 1% of the time
where the time goes in v3:
time: 220 us; the launch traced here: 219 us
  Pallas kernels  219 us (100%)
    pallas_call x1, Pallas kernels, forward(): pl.pallas_call(forward_kernel, grid=(2 * count,), in_specs=[smem, smem, p...  118 us
    pallas_call x1, Pallas kernels, backward(): pl.pallas_call(backward_kernel, grid=(20,), in_specs=[pl.BlockSpec(memory...  96 us
    pallas_call x1, Pallas kernels, emit(): pl.pallas_call(functools.partial(emit_kernel, len(large)), in_specs=[vmem...  4.89 us

profile of v3, /device:TPU:0, one launch (start us, length us, event | category | flops | bytes accessed | tf_op | source)
XLA Modules:
  0.0 219.5 jit_solution(8079089474647359754)
XLA Ops:
  0.7 117.8 %forward.1 = (bf16[1024,768]{1,0:T(8,128)(2,1)}, bf16[1024,2304]{1,0:T(8,128)(2,1)}, bf16[12,4,256,256]{3,2,1,0:T(8,128)(2,1)}, bf16[1024,768]{1,0:T(8,128)(2,1)...) custom-call(s32[4]{0:T(128)} %lengths.1, ...), custom_call_target="tpu_custom_call" | custom-call | tf_op jit(solution)/shard_map/forward/pallas_call | solution.py:932
  118.4 96.0 %backward.1 = (bf16[1024,768]{1,0:T(8,128)(2,1)}, f32[192,384]{1,0:T(8,128)}, f32[96,768]{1,0:T(8,128)}, f32[96,192]{1,0:T(8,128)}, f32[96,576]{1,0:T(8,128)}, /*index=5*/f32[16,384]{1,0:T(8,128)}) custom-call(s32[4]{0:T(128)} %buckets.3, bf16[1024,768]{1,0:T(8,128)(2,1)} %cot_hbm.1, bf16[1024,3072]{1,0:T(8,128)(2,1)} %get-tuple-element.61.act_ref, ...), custom_call_target="tpu_custom_call" | custom-call | tf_op jit(solution)/shard_map/backward/pallas_call | solution.py:1472
  214.4 4.9 %emit.1 = (bf16[1024,768]{1,0:T(8,128)(2,1)}, bf16[1024,768]{1,0:T(8,128)(2,1)}, f32[96,576]{1,0:T(8,128)}, f32[96,192]{1,0:T(8,128)}, f32[96,768]{1,0:T(8,128)}...) custom-call(f32[16,384]{1,0:T(8,128)} %get-tuple-element.75.total_re, ...), custom_call_target="tpu_custom_call" | custom-call | tf_op jit(solution)/shard_map/emit/pallas_call | solution.py:1564

commit v4 on v3

--- a/solution.py
+++ b/solution.py
@@ -309,7 +309,7 @@
     )(lengths, buckets, tokens, vecs, weight, qkv_bias, bias)
 
 
-PANEL = 512
+PANEL = 1024
 
 
 def feed_kernel(*refs):

time: 220 us -> 220 us (level)
  no operation moved by 1% of the time
where the time goes in v4:
time: 220 us
  Pallas kernels  219 us (100%)
    pallas_call x1, Pallas kernels, forward(): pl.pallas_call(forward_kernel, grid=(2 * count,), in_specs=[smem, smem, p...  118 us
    pallas_call x1, Pallas kernels, backward(): pl.pallas_call(backward_kernel, grid=(20,), in_specs=[pl.BlockSpec(memory...  96 us
    pallas_call x1, Pallas kernels, emit(): pl.pallas_call(functools.partial(emit_kernel, len(large)), in_specs=[vmem...  4.89 us

profile of v4, /device:TPU:0, one launch (start us, length us, event | category | flops | bytes accessed | tf_op | source)
XLA Modules:
  0.0 219.5 jit_solution(6977002542826031209)
XLA Ops:
  0.7 117.8 %forward.1 = (bf16[1024,768]{1,0:T(8,128)(2,1)}, bf16[1024,2304]{1,0:T(8,128)(2,1)}, bf16[12,4,256,256]{3,2,1,0:T(8,128)(2,1)}, bf16[1024,768]{1,0:T(8,128)(2,1)...) custom-call(s32[4]{0:T(128)} %lengths.1, ...), custom_call_target="tpu_custom_call" | custom-call | tf_op jit(solution)/shard_map/forward/pallas_call | solution.py:932
  118.5 96.0 %backward.1 = (bf16[1024,768]{1,0:T(8,128)(2,1)}, f32[192,384]{1,0:T(8,128)}, f32[96,768]{1,0:T(8,128)}, f32[96,192]{1,0:T(8,128)}, f32[96,576]{1,0:T(8,128)}, /*index=5*/f32[16,384]{1,0:T(8,128)}) custom-call(s32[4]{0:T(128)} %buckets.3, bf16[1024,768]{1,0:T(8,128)(2,1)} %cot_hbm.1, bf16[1024,3072]{1,0:T(8,128)(2,1)} %get-tuple-element.61.act_ref, ...), custom_call_target="tpu_custom_call" | custom-call | tf_op jit(solution)/shard_map/backward/pallas_call | solution.py:1472
  214.5 4.9 %emit.1 = (bf16[1024,768]{1,0:T(8,128)(2,1)}, bf16[1024,768]{1,0:T(8,128)(2,1)}, f32[96,576]{1,0:T(8,128)}, f32[96,192]{1,0:T(8,128)}, f32[96,768]{1,0:T(8,128)}...) custom-call(f32[16,384]{1,0:T(8,128)} %get-tuple-element.75.total_re, ...), custom_call_target="tpu_custom_call" | custom-call | tf_op jit(solution)/shard_map/emit/pallas_call | solution.py:1564
